TPU v7x, 128 devices: a whole 4x4x4 slice. The times are simulated.
128 devices in a mesh: grp: 8 (over x, core), head: 16 (over z, y).
Axes of the slice: x: 4, y: 4, z: 4, core: 2. Of those that a mesh axis runs over, the one named last changes fastest.
Arguments:
- request_owner: int32 [256], P('grp'), parts along dimension 0, may hold values from 0 to 15, as said below
- page_list: int32 [256, 8], P('grp'), parts along dimension 0, may hold values from 0 to 255, as said below
- context_len: int32 [256], P('grp'), parts along dimension 0, may hold values from 1 to 1024, as said below
- lin_state: float32 [256, 64, 128, 128], P('grp', 'head'), parts along dimension 0, may hold values from -6 to 6
- decay_rate: float32 [64], replicated, may hold values from 0.02 to 3
- lin_query: bfloat16 [256, 2, 8192], P(('grp', 'head')), parts along dimension 0, may hold values from -0.5 to 0.5
- lin_keyval: bfloat16 [256, 2, 2, 8192], P(('grp', 'head')), parts along dimension 0, may hold values from -5 to 5
- soft_query: bfloat16 [256, 2, 8192], P(('grp', 'head')), parts along dimension 0, may hold values from -10 to 10
- new_keyval: bfloat16 [256, 2, 2, 1024], P(('grp', 'head')), parts along dimension 0, may hold values from -4 to 4
- page_pool: bfloat16 [2048, 2, 128, 1024], P(('grp', 'head')), parts along dimension 0, may hold values from -4 to 4
Outputs:
- lin_out: float32 [256, 2, 8192], P(('grp', 'head')), parts along dimension 0
- soft_out: float32 [256, 2, 8192], P(('grp', 'head')), parts along dimension 0
There are 8 independent parts, one for each index of `grp`. A program takes and returns all parts, laid end to end along the dimension named above; an argument that names none is the same for every part. Nothing has to cross between parts.
Inputs may be any that keep to these rules, and one draw needn't show every extreme that they name: `request_owner`: each owner 0 .. 15 names exactly 2 requests. `page_list`: all entries of the table are distinct, so every pool page is listed once. Pages 16 * d .. 16 * d + 15 lie on device d of head; among them at most 2 are listed by the requests of one owner, exactly 2 for some device and owner. Entries j with j * 128 >= context_len of the request are padding. `context_len`: some request has exactly 1024 cached tokens.
All inputs are finite; a program needn't handle non-finite values.
Results may differ from a plain program's by a relative error of at most 0.0012.
Values may be sent and summed in bfloat16 or wider, within the bound.
A program may use at most 128 MiB of HBM per device.

v0:
```python
import math

import jax
import jax.numpy as jnp
from jax import lax
from jax.sharding import PartitionSpec as P


def row_tables(request_owner, per_owner):
    total = request_owner.shape[0]
    index = jnp.arange(total, dtype=jnp.int32)
    same = request_owner[:, None] == request_owner[None, :]
    earlier = index[None, :] < index[:, None]
    slots = jnp.sum(jnp.where(same & earlier, 1, 0), axis=1).astype(jnp.int32)
    row_of = request_owner * per_owner + slots
    match = row_of[None, :] == index[:, None]
    request_of = jnp.sum(jnp.where(match, index[None, :], 0), axis=1)
    return (row_of, request_of)


def lightning(state, query, keyval, rates):
    batch, heads_n, width = (state.shape[0], state.shape[1], state.shape[2])
    factor = jnp.exp(-rates)[None, :, None, None]
    outputs = []
    for step in range(keyval.shape[1]):
        keys = keyval[:, step, 0].astype(jnp.float32).reshape(batch, heads_n, width)
        values = keyval[:, step, 1].astype(jnp.float32).reshape(batch, heads_n, width)
        state = factor * state + keys[:, :, :, None] * values[:, :, None, :]
        query_now = query[:, step].astype(jnp.float32).reshape(batch, heads_n, width)
        mixed = jnp.einsum("bhd,bhde->bhe", query_now, state, precision=lax.Precision.HIGHEST)
        spread = jnp.sqrt(jnp.mean(mixed * mixed, axis=-1, keepdims=True) + 1e-05)
        outputs.append((mixed / spread).reshape(batch, heads_n * width))
    return jnp.stack(outputs, axis=1)


def page_partial(query, keys, values, live):
    scores = jnp.einsum("tkgd,nkd->tkgn", query, keys, preferred_element_type=jnp.float32) * (
        1.0 / math.sqrt(query.shape[-1])
    )
    mask = live[:, None, None, :]
    top = jnp.max(jnp.where(mask, scores, -1e30), axis=-1)
    weights = jnp.where(mask, jnp.exp(scores - top[..., None]), 0.0)
    total = jnp.sum(weights, axis=-1)
    rounded = weights.astype(jnp.bfloat16)
    acc = jnp.einsum("tkgn,nkd->tkgd", rounded, values, preferred_element_type=jnp.float32)
    return (top, total, acc)


def merge_blocks(tops, totals, accs, axis):
    peak = jnp.max(tops, axis=axis, keepdims=True)
    factor = jnp.exp(tops - peak)
    denom = jnp.sum(factor * totals, axis=axis)
    numer = jnp.sum(factor[..., None] * accs, axis=axis)
    return numer / denom[..., None]


def shards(
    request_owner,
    page_list,
    context_len,
    lin_state,
    decay_rate,
    lin_query,
    lin_keyval,
    soft_query,
    new_keyval,
    page_pool,
):
    devices = lax.axis_size("head")
    device_id = lax.axis_index("head")
    total = request_owner.shape[0]
    per_owner = total // devices
    width = lin_state.shape[2]
    heads_all = decay_rate.shape[0]
    kvh = new_keyval.shape[-1] // width
    group = heads_all // kvh
    steps = soft_query.shape[1]
    span = page_list.shape[1]
    own_pages = page_pool.shape[0]
    pair_cap = 2 * own_pages // devices
    page_size = page_pool.shape[2]
    row_of, request_of = row_tables(request_owner, per_owner)
    ordered = jnp.take(lin_state, request_of, axis=0)
    owned_state = lax.all_to_all(ordered, "head", split_axis=0, concat_axis=1, tiled=True)
    lin_out = lightning(owned_state, lin_query, lin_keyval, decay_rate)
    row_pages = jnp.take(page_list, request_of, axis=0).reshape(devices, own_pages)
    holder = row_pages // own_pages
    local_index = row_pages % own_pages
    row_len = jnp.take(context_len, request_of, axis=0)
    slot_index = jnp.arange(own_pages, dtype=jnp.int32)
    slot_row = (
        jnp.arange(devices, dtype=jnp.int32)[:, None] * per_owner + slot_index[None, :] // span
    )
    slot_page = slot_index % span
    slot_count = jnp.clip(
        jnp.take(row_len, slot_row, axis=0) - slot_page[None, :] * page_size, 0, page_size
    )
    my_holder = lax.dynamic_index_in_dim(holder, device_id, 0, keepdims=False)
    same_holder = my_holder[:, None] == my_holder[None, :]
    before = slot_index[None, :] < slot_index[:, None]
    my_position = my_holder * pair_cap + jnp.sum(jnp.where(same_holder & before, 1, 0), axis=1)
    my_count = lax.dynamic_index_in_dim(slot_count, device_id, 0, keepdims=False)
    held_here = holder == device_id
    rank = jnp.cumsum(held_here.astype(jnp.int32), axis=1) - 1
    picked = held_here[:, None, :] & (
        rank[:, None, :] == jnp.arange(pair_cap, dtype=jnp.int32)[None, :, None]
    )
    send_local = jnp.sum(jnp.where(picked, local_index[:, None, :], 0), axis=-1).reshape(-1)

    def page_block(query, page, count):
        grouped = query.reshape(steps, kvh, group, width)
        live = jnp.broadcast_to(
            jnp.arange(page_size, dtype=jnp.int32)[None, :] < count, (steps, page_size)
        )
        return page_partial(
            grouped,
            page[0].reshape(page_size, kvh, width),
            page[1].reshape(page_size, kvh, width),
            live,
        )

    outgoing = jnp.take(page_pool, send_local, axis=0)
    arrived = lax.all_to_all(outgoing, "head", split_axis=0, concat_axis=0, tiled=True)
    my_pages = jnp.take(arrived, my_position, axis=0)
    slot_query = jnp.repeat(soft_query, span, axis=0)
    tops, totals, accs = jax.vmap(page_block)(slot_query, my_pages, my_count)
    live_new = jnp.arange(steps)[None, :] <= jnp.arange(steps)[:, None]

    def fresh_block(query, fresh):
        grouped = query.reshape(steps, kvh, group, width)
        return page_partial(
            grouped,
            fresh[:, 0].reshape(steps, kvh, width),
            fresh[:, 1].reshape(steps, kvh, width),
            live_new,
        )

    top_new, total_new, acc_new = jax.vmap(fresh_block)(soft_query, new_keyval)
    tops = jnp.concatenate(
        [tops.reshape((per_owner, span) + tops.shape[1:]), top_new[:, None]], axis=1
    )
    totals = jnp.concatenate(
        [totals.reshape((per_owner, span) + totals.shape[1:]), total_new[:, None]], axis=1
    )
    accs = jnp.concatenate(
        [accs.reshape((per_owner, span) + accs.shape[1:]), acc_new[:, None]], axis=1
    )
    soft_out = merge_blocks(tops, totals, accs, 1).reshape(per_owner, steps, heads_all * width)
    return (lin_out, soft_out)


def solution(mesh):
    return jax.shard_map(
        shards,
        mesh=mesh,
        in_specs=(
            P("grp"),
            P("grp", None),
            P("grp"),
            P("grp", "head", None, None),
            P(),
            P(("grp", "head"), None, None),
            P(("grp", "head"), None, None, None),
            P(("grp", "head"), None, None),
            P(("grp", "head"), None, None, None),
            P(("grp", "head"), None, None, None),
        ),
        out_specs=(P(("grp", "head"), None, None), P(("grp", "head"), None, None)),
        check_vma=False,
    )
```

profile of v0, /device:TPU:0, one launch (start us, length us, event | category | flops | bytes accessed | tf_op | source)
XLA Modules:
  0.0 448.2 jit_solution(15298353265120984624)
XLA Ops:
  0.6 0.9 select_reduce_fusion.4
  1.6 0.7 multiply_add_fusion.3
  2.4 0.7 gather_fusion.1
  3.1 7.7 %gather_fusion = f32[32,4,128,128]{3,2,1,0:T(8,128)} fusion(f32[32,4,128,128]{3,2,1,0:T(8,128)} %param.13, s32[1024]{0:T(1024)S(1)} %pad_clamp_fusion.3), kind=kCustom, calls=%fused_computation | custom fusion | bytes 16777344 | tf_op jit(solution)/shard_map/jit(_take)/gather | solution.py:83
  10.8 8.4 %broadcast_select_fusion.2 = f32[32,4,128,128]{3,2,1,0:T(8,128)} fusion(f32[32,4,128,128]{3,2,1,0:T(8,128)} %gather_fusion, pred[32]{0:T(512)(128)(4,1)S(1)} %get-tuple-element.7), kind=kLoop, calls=%fused_computation.20 | loop fusion | flops 2097152 | bytes 16777248 | tf_op jit(solution)/shard_map/jit(_take)/select_n | solution.py:83
  19.2 8.3 %all-to-all-start = ((f32[32,4,128,128]{3,2,1,0:T(8,128)}), f32[32,4,128,128]{3,2,1,0:T(8,128)}, u32[]{:S(2)}, u32[]{:S(2)}) async-start(f32[32,4,128,128]{3,2,1,0:T(8,128)} %broadcast_select_fusion.2), calls=%async_computation | async-start | bytes 16777216 | tf_op jit(solution)/shard_map/all_to_all | solution.py:84
  27.7 0.6 gather_fusion.3
  29.2 10.5 %gather_fusion.4 = bf16[32,2,128,1024]{3,2,1,0:T(8,128)(2,1)} fusion(bf16[16,2,128,1024]{3,2,1,0:T(8,128)(2,1)} %param.19, s32[1024]{0:T(1024)S(1)} %pad_clamp_fusion.1), kind=kCustom, calls=%fused_computation.4 | custom fusion | bytes 33554560 | tf_op jit(solution)/shard_map/jit(_take)/gather | solution.py:122
  39.7 14.2 %broadcast_select_fusion = bf16[32,2,128,1024]{3,2,1,0:T(8,128)(2,1)} fusion(bf16[32,2,128,1024]{3,2,1,0:T(8,128)(2,1)} %gather_fusion.4, pred[32]{0:T(512)(128)(4,1)S(1)} %compare_and_fusion.1), kind=kLoop, calls=%fused_computation.6 | loop fusion | flops 8388608 | bytes 33554464 | tf_op jit(solution)/shard_map/jit(_take)/select_n | solution.py:122
  53.9 97.7 %all-to-all-done = f32[32,4,128,128]{3,2,1,0:T(8,128)} async-done(((f32[32,4,128,128]{3,2,1,0:T(8,128)}), f32[32,4,128,128]{3,2,1,0:T(8,128)}, u32[]{:S(2)}, u32[]{:S(2)}) %all-to-all-start) | async-done | bytes 8388640 | tf_op jit(solution)/shard_map/all_to_all | solution.py:84
  151.5 5.7 %all-to-all-start.1 = ((bf16[32,2,128,1024]{3,2,1,0:T(8,128)(2,1)}), bf16[32,2,128,1024]{3,2,1,0:T(8,128)(2,1)}, u32[]{:S(2)}, u32[]{:S(2)}) async-start(bf16[32,2,128,1024]{3,2,1,0:T(8,128)(2,1)} %broadcast_select_fusion), calls=%async_computation.1 | async-start | bytes 33554432 | tf_op jit(solution)/shard_map/all_to_all | solution.py:123
  157.7 1.9 gather_fusion.2
  160.0 0.2 select_reduce_fusion.5
  160.2 0.4 select_reduce_fusion.1
  160.7 0.3 convolution_bitcast_fusion
  161.3 0.2 slice_convert_fusion.3
  161.5 4.0 copy.72
  165.5 9.8 %fusion = f32[2,64,1,128]{3,2,1,0:T(1,128)S(1)} fusion(f32[2,64,128,128]{3,2,1,0:T(8,128)S(1)} %bitcast.85, f32[2,64,128]{2,1,0:T(8,128)S(1)} %bitcast.105, f32[2,64,128]{2,1,0:T(8,128)S(1)} %bitcast.106, f32[2,64,128]{2,1,0:T(8,128)S(1)} %bitcast.98, f32[2,64,128]{2,1,0:T(8,128)S(1)} %bitcast.96, f32[64]{0:T(128)S(1)} %negate_exponential_fusion, ...), kind=kOutput, calls=%fused_computation.7 | convolution fusion | flops 37748736 | bytes 8782080 | tf_op jit(solution)/shard_map/bhd,bhde->bhe/dot_general | solution.py:30
  175.4 5.4 %fusion.4 = f32[2,64,1,128]{3,2,1,0:T(1,128)S(1)} fusion(f32[2,64,128,128]{3,2,1,0:T(8,128)S(1)} %bitcast.86, f32[2,64,128]{2,1,0:T(8,128)S(1)} %bitcast.99, f32[2,64,128]{2,1,0:T(8,128)S(1)} %bitcast.97, f32[64]{0:T(128)S(1)} %negate_exponential_fusion, bf16[2,2,8192]{2,1,0:T(2,128)(2,1)S(1)} %copy-done.4), kind=kOutput, calls=%fused_computation.13 | convolution fusion | flops 31457280 | bytes 8651008 | tf_op jit(solution)/shard_map/bhd,bhde->bhe/dot_general | solution.py:30
  181.1 0.8 pad_maximum_fusion
  181.9 219.2 %all-to-all-done.1 = bf16[32,2,128,1024]{3,2,1,0:T(8,128)(2,1)} async-done(((bf16[32,2,128,1024]{3,2,1,0:T(8,128)(2,1)}), bf16[32,2,128,1024]{3,2,1,0:T(8,128)(2,1)}, u32[]{:S(2)}, u32[]{:S(2)}) %all-to-all-start.1) | async-done | bytes 16777248 | tf_op jit(solution)/shard_map/all_to_all | solution.py:123
  401.1 10.5 %gather_fusion.5 = bf16[16,2,128,1024]{3,2,1,0:T(8,128)(2,1)} fusion(bf16[32,2,128,1024]{3,2,1,0:T(8,128)(2,1)} %all-to-all-done.1, s32[1024]{0:T(1024)S(1)} %pad_clamp_fusion), kind=kCustom, calls=%fused_computation.5 | custom fusion | bytes 16777280 | tf_op jit(solution)/shard_map/jit(_take)/gather | solution.py:124
  411.6 7.5 %broadcast_select_fusion.1 = bf16[16,2,128,1024]{3,2,1,0:T(8,128)(2,1)} fusion(bf16[16,2,128,1024]{3,2,1,0:T(8,128)(2,1)} %gather_fusion.5, pred[16]{0:T(512)(128)(4,1)S(1)} %compare_and_fusion.2), kind=kLoop, calls=%fused_computation.12 | loop fusion | flops 4194304 | bytes 16777232 | tf_op jit(solution)/shard_map/jit(_take)/select_n | solution.py:124
  419.1 6.0 %fusion.48 = (bf16[16,1,128,1024]{3,2,1,0:T(8,128)(2,1)}, bf16[16,1,128,1024]{3,2,1,0:T(8,128)(2,1)}) fusion(bf16[16,2,128,1024]{3,2,1,0:T(8,128)(2,1)} %broadcast_select_fusion.1), kind=kLoop, calls=%fused_computation.137 | loop fusion | bytes 16777216 | tf_op jit(solution)/shard_map/vmap()/slice | solution.py:117
  425.1 6.4 %copy.78 = bf16[16,1,128,1024]{2,3,0,1:T(8,128)(2,1)} copy(bf16[16,1,128,1024]{3,2,1,0:T(8,128)(2,1)} %get-tuple-element.11) | data formatting | bytes 8388608 | tf_op jit(solution)/shard_map/vmap()/slice | solution.py:117
  431.4 3.5 select_reduce_fusion
  435.1 0.8 fusion.16
  435.9 6.4 %copy.84 = bf16[16,1,128,1024]{2,3,0,1:T(8,128)(2,1)} copy(bf16[16,1,128,1024]{3,2,1,0:T(8,128)(2,1)} %get-tuple-element.12) | data formatting | bytes 8388608 | tf_op jit(solution)/shard_map/vmap()/slice | solution.py:118
  442.3 4.5 %fusion.18 = f32[16,8,128,2,8]{2,4,3,1,0:T(8,128)S(1)} fusion(bf16[16,128,8,128,1]{1,3,4,2,0:T(8,128)(2,1)} %bitcast.88, f32[16,2,8,8,128]{4,3,1,2,0:T(8,128)S(1)} %get-tuple-element.22, f32[16,2,8,8]{3,1,2,0:T(2,128)S(1)} %get-tuple-element.21, pred[16,128]{1,0:T(8,128)(4,1)S(1)} %iota_compare_fusion.4), kind=kOutput, calls=%fused_computation.34 | convolution fusion | flops 67895296 | bytes 6301696 | tf_op jit(solution)/shard_map/vmap(tkgn,nkd->tkgd)/dot_general | solution.py:45
  446.8 0.2 fusion.25
  447.0 0.4 fusion.14
  447.5 0.7 div.70
  (72 shorter events, 2.9 us)
Async XLA Ops:
  0.6 1.7 copy-start
  19.2 8.4 %copy-start.6 = (s32[32,8]{0,1:T(8,128)S(1)}, s32[32,8]{0,1:T(8,128)}, u32[]{:S(2)}) copy-start(s32[32,8]{0,1:T(8,128)} %param.11) | copy-start | bytes 3076
  19.2 132.3 %all-to-all-start = ((f32[32,4,128,128]{3,2,1,0:T(8,128)}), f32[32,4,128,128]{3,2,1,0:T(8,128)}, u32[]{:S(2)}, u32[]{:S(2)}) async-start(f32[32,4,128,128]{3,2,1,0:T(8,128)} %broadcast_select_fusion.2), calls=%async_computation | async-start | bytes 16777216 | tf_op jit(solution)/shard_map/all_to_all | solution.py:84
  53.9 103.5 %copy-start.3 = (bf16[2,2,8192]{2,1,0:T(2,128)(2,1)S(1)}, bf16[2,2,8192]{2,1,0:T(2,128)(2,1)}, u32[]{:S(2)}) copy-start(bf16[2,2,8192]{2,1,0:T(2,128)(2,1)} %param.17) | copy-start | bytes 196612
  151.5 249.5 %all-to-all-start.1 = ((bf16[32,2,128,1024]{3,2,1,0:T(8,128)(2,1)}), bf16[32,2,128,1024]{3,2,1,0:T(8,128)(2,1)}, u32[]{:S(2)}, u32[]{:S(2)}) async-start(bf16[32,2,128,1024]{3,2,1,0:T(8,128)(2,1)} %broadcast_select_fusion), calls=%async_computation.1 | async-start | bytes 33554432 | tf_op jit(solution)/shard_map/all_to_all | solution.py:123
  157.3 2.5 copy-start.5
  157.3 3.7 copy-start.7
  157.3 4.0 copy-start.2
  161.5 4.0 copy-start.4
  435.8 12.4 %copy-start.1 = (s32[32]{0:T(128)S(1)}, s32[32]{0:T(128)}, u32[]{:S(2)}) copy-start(s32[32]{0:T(128)} %param.12) | copy-start | bytes 388
where the time goes:
time: 449 us; the launch traced here: 448 us
  waiting for transfers between devices  317 us (71%)
  local copies, waits for them, and re-layouts  56.7 us (13%)
  other arithmetic  35.7 us (8%)
  matrix products  23.9 us (5%)
  starting transfers between devices  14.1 us (3%)
    all_to_all x1, waiting for transfers between devices, shards(): lax.all_to_all(outgoing, 'head', split_axis=0, concat_axis=0, tiled=True)  219 us
    all_to_all x1, waiting for transfers between devices, shards(): lax.all_to_all(ordered, 'head', split_axis=0, concat_axis=1, tiled=True)  97.7 us
    dot_general x2, matrix products, lightning(): jnp.einsum('bhd,bhde->bhe', query_now, state, precision=lax.Precision.HIG...  15.2 us
    select_n x2, other arithmetic, shards(): outgoing = jnp.take(page_pool, send_local, axis=0)  14.2 us
    slice x2, local copies, waits for them, and re-layouts, page_block(): page[0].reshape(page_size, kvh, width)  12.4 us
    gather x1, local copies, waits for them, and re-layouts, shards(): my_pages = jnp.take(arrived, my_position, axis=0)  10.5 us
    gather x1, local copies, waits for them, and re-layouts, shards(): outgoing = jnp.take(page_pool, send_local, axis=0)  10.5 us
  transfers between devices with their start and end apart: 2, of which 2 were waited for; matrix products, arithmetic and copies ran while one was open for 11% of the time, Pallas kernels for 0%

commit v1 on v0

v1 whole, which is shorter than its diff:
```python
import functools
import math

import jax
import jax.numpy as jnp
from jax import lax
from jax.experimental import pallas as pl
from jax.experimental.pallas import tpu as pltpu
from jax.sharding import PartitionSpec as P

MESH = pl.DeviceIdType.MESH
N = 16
WIDTH = 128
KVH = 8
CODES = 32000.0
LOW = -1e30
SCALE = 1.0 / math.sqrt(128.0)


def tables(request_owner, page_list, context_len, me):
    total = request_owner.shape[0]
    index = jnp.arange(total, dtype=jnp.int32)
    same = request_owner[:, None] == request_owner[None, :]
    earlier = index[None, :] < index[:, None]
    slots = jnp.sum(jnp.where(same & earlier, 1, 0), axis=1).astype(jnp.int32)
    row_of = request_owner * 2 + slots
    request_of = jnp.sum(jnp.where(row_of[None, :] == index[:, None], index[None, :], 0), axis=1)
    span = page_list.shape[1]
    here = page_list // 16 == me
    entry = row_of[:, None] * span + jnp.arange(span, dtype=jnp.int32)[None, :]
    count = jnp.clip(context_len[:, None] - jnp.arange(span, dtype=jnp.int32)[None, :] * WIDTH, 0, WIDTH)
    here, entry, count = here.reshape(-1), entry.reshape(-1), count.reshape(-1)
    local = (page_list % 16).reshape(-1)
    before = here[None, :] & (entry[None, :] // 16 == entry[:, None] // 16) & (entry[None, :] < entry[:, None])
    slot = jnp.where(here, entry // 16 * 2 + jnp.sum(jnp.where(before, 1, 0), axis=1), -1)
    packed = local + entry // 8 % 2 * 16 + count * 32
    slot_codes = jnp.sum(
        jnp.where(slot[None, :] == jnp.arange(2 * N, dtype=jnp.int32)[:, None], packed[None, :], 0), axis=1
    )
    return jnp.concatenate([request_of, slot_codes]).astype(jnp.int32)


def kernel(
    tab, rate, lq, lkv, sq, nkv, state_hbm, pool_hbm, lin_ref, soft_ref,
    state, pool, q_all, lq_in, lkv_in, lin_send, lin_in, res_send, res_in, meta_send, meta_in, run_acc, run_meta,
    local_sem, send_sem, recv_sem,
):
    me = lax.axis_index("head")
    mz, my = me // 4, me % 4

    def ahead(i):
        return (mz + i // 4) % 4 * 4 + (my + i % 4) % 4

    def behind(i):
        return (mz + 4 - i // 4) % 4 * 4 + (my + 4 - i % 4) % 4

    def remote(src, dst, kind, i, to):
        return pltpu.make_async_remote_copy(
            src_ref=src, dst_ref=dst, send_sem=send_sem.at[kind, i], recv_sem=recv_sem.at[kind, i],
            device_id={"head": to}, device_id_type=MESH,
        )

    def lin_part(i):
        to = ahead(i)
        lanes = pl.ds(pl.multiple_of(to * 512, 512), 512)
        return (
            remote(lq.at[:, :, lanes], lq_in.at[i], 0, i, to),
            remote(lkv.at[:, :, :, lanes], lkv_in.at[i], 1, i, to),
        )

    def query(i):
        return remote(q_all.at[0], q_all.at[i], 2, i, ahead(i))

    def lin_back(i):
        return remote(lin_send.at[i], lin_in.at[me], 3, i, behind(i))

    def result(i):
        return remote(res_send.at[i], res_in.at[i], 4, i, behind(i))

    def meta(i):
        return remote(meta_send.at[i], meta_in.at[i], 5, i, behind(i))

    barrier = pltpu.get_barrier_semaphore()

    def greet(i, carry):
        pl.semaphore_signal(barrier, inc=1, device_id={"head": ahead(i)}, device_id_type=MESH)
        return carry

    lax.fori_loop(1, N, greet, 0)
    fetch_state = pltpu.make_async_copy(state_hbm, state, local_sem.at[0])
    fetch_pool = pltpu.make_async_copy(pool_hbm, pool, local_sem.at[1])
    fetch_state.start()
    fetch_pool.start()
    own_lanes = pl.ds(pl.multiple_of(me * 512, 512), 512)
    own_q = pltpu.make_async_copy(lq.at[:, :, own_lanes], lq_in.at[0], local_sem.at[2])
    own_kv = pltpu.make_async_copy(lkv.at[:, :, :, own_lanes], lkv_in.at[0], local_sem.at[3])
    own_q.start()
    own_kv.start()
    for r in range(2):
        wide = sq[r].astype(jnp.float32)
        q_all[0, r] = jnp.concatenate(
            [wide[:, h * WIDTH:(h + 1) * WIDTH] for h in range(64)], axis=0
        ).astype(jnp.bfloat16)
    pl.semaphore_wait(barrier, N - 1)

    def send_lin(i, carry):
        a, b = lin_part(i)
        a.start()
        b.start()
        return carry

    def send_query(i, carry):
        query(i).start()
        return carry

    lax.fori_loop(1, N, send_lin, 0)
    lax.fori_loop(1, N, send_query, 0)
    own_q.wait()
    own_kv.wait()
    fetch_state.wait()

    row8 = lax.broadcasted_iota(jnp.int32, (8, 64), 0)
    lane8 = lax.broadcasted_iota(jnp.int32, (8, 64), 1)
    rates = jnp.sum(jnp.where(lane8 == me * 4 + row8 // 2, rate[...], 0.0), axis=1, keepdims=True)
    second = lax.broadcasted_iota(jnp.int32, (8, 1), 0) % 2 == 1
    lam = jnp.exp(-rates)
    lam_state = jnp.where(second, lam * lam, lam)
    lam_first = jnp.where(second, lam, 1.0)
    lam_second = jnp.where(second, 1.0, 0.0)
    head_of = lax.broadcasted_iota(jnp.int32, (8, WIDTH), 0) // 2

    def spread(x):
        return jnp.concatenate(
            [jnp.broadcast_to(x[:, h * WIDTH:(h + 1) * WIDTH], (2, WIDTH)) for h in range(4)], axis=0
        )

    def lightning(i, carry):
        owner = behind(i)

        @pl.when(i > 0)
        def _():
            a, b = lin_part(i)
            a.wait_recv()
            b.wait_recv()

        for r in range(2):
            request = tab[owner * 2 + r]
            q = lq_in[i, r].astype(jnp.float32)
            q = jnp.concatenate([q[:, h * WIDTH:(h + 1) * WIDTH] for h in range(4)], axis=0)
            kv1 = lkv_in[i, r, 0].astype(jnp.float32)
            kv2 = lkv_in[i, r, 1].astype(jnp.float32)
            q_bf = q.astype(jnp.bfloat16)
            q_two = jnp.concatenate([q_bf, q_bf], axis=1)
            y = jnp.zeros((8, WIDTH), jnp.float32)
            for h in range(4):
                s = state[request, h]
                high = s.astype(jnp.bfloat16)
                low = (s - high.astype(jnp.float32)).astype(jnp.bfloat16)
                got = jnp.dot(q_two, jnp.concatenate([high, low], axis=0), preferred_element_type=jnp.float32)
                y = jnp.where(head_of == h, got, y)
            k1, v1, k2, v2 = spread(kv1[0:1]), spread(kv1[1:2]), spread(kv2[0:1]), spread(kv2[1:2])
            qk1 = jnp.sum(q * k1, axis=1, keepdims=True)
            qk2 = jnp.sum(q * k2, axis=1, keepdims=True)
            y = lam_state * y + (lam_first * qk1) * v1 + (lam_second * qk2) * v2
            norm = jnp.sqrt(jnp.mean(y * y, axis=1, keepdims=True) + 1e-5)
            lin_send[i, r] = y / norm

        @pl.when(i > 0)
        def _():
            lin_back(i).start()

        return carry

    lax.fori_loop(0, N, lightning, 0)
    fetch_pool.wait()

    eye = lax.broadcasted_iota(jnp.int32, (WIDTH, WIDTH), 0) == lax.broadcasted_iota(jnp.int32, (WIDTH, WIDTH), 1)
    position = lax.broadcasted_iota(jnp.int32, (WIDTH, WIDTH), 1)

    def as_row(column):
        return jnp.sum(jnp.where(eye, column, 0.0), axis=0, keepdims=True)

    def softmax(i, carry):
        owner = behind(i)

        @pl.when(i > 0)
        def _():
            query(i).wait_recv()

        found = []
        for k in range(2):
            code = tab[32 + owner * 2 + k]
            page, row, count = code % 16, code // 16 % 2, code // 32
            live = position < count
            q = jnp.where(row == 1, q_all[i, 1], q_all[i, 0])
            scores = jnp.concatenate(
                [
                    lax.dot_general(
                        q[c * 16:(c + 1) * 16], pool[page, 0, :, c * WIDTH:(c + 1) * WIDTH],
                        (((1,), (1,)), ((), ())), preferred_element_type=jnp.float32,
                    )
                    for c in range(KVH)
                ],
                axis=0,
            ) * SCALE
            top = jnp.max(jnp.where(live, scores, LOW), axis=1, keepdims=True)
            weight = jnp.where(live, jnp.exp(scores - top), 0.0)
            total = jnp.sum(weight, axis=1, keepdims=True)
            rounded = weight.astype(jnp.bfloat16)
            acc = jnp.concatenate(
                [
                    jnp.dot(
                        rounded[c * 16:(c + 1) * 16], pool[page, 1, :, c * WIDTH:(c + 1) * WIDTH],
                        preferred_element_type=jnp.float32,
                    )
                    for c in range(KVH)
                ],
                axis=0,
            )
            found.append((row, top, total, acc))
        metas = []
        for r in range(2):
            tops = [jnp.where(row == r, top, LOW) for row, top, _, _ in found]
            peak = jnp.maximum(tops[0], tops[1])
            factors = [
                jnp.where(row == r, jnp.exp(t - peak), 0.0) for t, (row, _, _, _) in zip(tops, found)
            ]
            total = factors[0] * found[0][2] + factors[1] * found[1][2]
            acc = factors[0] * found[0][3] + factors[1] * found[1][3]
            most = jnp.maximum(jnp.max(jnp.abs(acc), axis=1, keepdims=True), 1e-30)
            coded = (acc * (CODES / most) + 32768.5).astype(jnp.int32)
            res_send[i, r] = lax.shift_left(coded[:64], 16) | coded[64:]
            metas += [as_row(peak), as_row(total), as_row(most * (1.0 / CODES))]
        zero = jnp.zeros((2, WIDTH), jnp.float32)
        meta_send[i] = jnp.concatenate(metas + [zero], axis=0)

        @pl.when(i > 0)
        def _():
            result(i).start()
            meta(i).start()

        return carry

    lax.fori_loop(0, N, softmax, 0)

    keep = [
        pltpu.make_async_copy(lin_send.at[0], lin_in.at[me], local_sem.at[4]),
        pltpu.make_async_copy(res_send.at[0], res_in.at[0], local_sem.at[5]),
        pltpu.make_async_copy(meta_send.at[0], meta_in.at[0], local_sem.at[6]),
    ]
    for copy in keep:
        copy.start()

    step = lax.broadcasted_iota(jnp.int32, (WIDTH, 1), 0) % 2

    def by_head(x):
        return jnp.concatenate(
            [jnp.broadcast_to(x[:, c * WIDTH:(c + 1) * WIDTH], (16, WIDTH)) for c in range(KVH)], axis=0
        )

    for r in range(2):
        q = q_all[0, r].astype(jnp.float32)
        kv = [nkv[r, t].astype(jnp.float32) for t in range(2)]
        s0 = jnp.sum(q * by_head(kv[0][0:1]), axis=1, keepdims=True) * SCALE
        s1 = jnp.sum(q * by_head(kv[1][0:1]), axis=1, keepdims=True) * SCALE
        top = jnp.where(step == 1, jnp.maximum(s0, s1), s0)
        w0 = jnp.exp(s0 - top)
        w1 = jnp.where(step == 1, jnp.exp(s1 - top), 0.0)
        r0 = w0.astype(jnp.bfloat16).astype(jnp.float32)
        r1 = w1.astype(jnp.bfloat16).astype(jnp.float32)
        run_acc[r] = r0 * by_head(kv[0][1:2]) + r1 * by_head(kv[1][1:2])
        run_meta[r, 0] = jnp.broadcast_to(top, (WIDTH, WIDTH))
        run_meta[r, 1] = jnp.broadcast_to(w0 + w1, (WIDTH, WIDTH))
    for copy in keep:
        copy.wait()

    def merge(i, carry):
        @pl.when(i > 0)
        def _():
            result(i).wait_recv()
            meta(i).wait_recv()

        columns = jnp.concatenate([meta_in[i], jnp.zeros((WIDTH - 8, WIDTH), jnp.float32)], axis=0).T
        for r in range(2):
            top, total, scale = (columns[:, 3 * r + n:3 * r + n + 1] for n in range(3))
            old = run_meta[r, 0][:, 0:1]
            peak = jnp.maximum(old, top)
            mine, theirs = jnp.exp(old - peak), jnp.exp(top - peak)
            words = res_in[i, r]
            first = lax.shift_right_logical(words, 16).astype(jnp.float32)
            later = (words & 65535).astype(jnp.float32)
            codes = jnp.concatenate([first, later], axis=0) - 32768.0
            run_acc[r] = mine * run_acc[r] + (theirs * scale) * codes
            run_meta[r, 1] = mine * run_meta[r, 1] + theirs * total
            run_meta[r, 0] = jnp.broadcast_to(peak, (WIDTH, WIDTH))
        return carry

    lax.fori_loop(0, N, merge, 0)
    for r in range(2):
        soft_ref[r] = run_acc[r] / run_meta[r, 1]

    def finish(i, carry):
        a, b = lin_part(i)
        a.wait_send()
        b.wait_send()
        query(i).wait_send()
        back = lin_back(i)
        back.wait_send()
        back.wait_recv()
        result(i).wait_send()
        meta(i).wait_send()
        return carry

    lax.fori_loop(1, N, finish, 0)

    def place(i, carry):
        for r in range(2):
            lin_ref[r, pl.ds(pl.multiple_of(i * 8, 8), 8)] = lin_in[i, r]
        return carry

    lax.fori_loop(0, N, place, 0)


def rows_last(x):
    return x.reshape(2, 64, 2, WIDTH).transpose(0, 2, 1, 3).reshape(2, 2, 64 * WIDTH)


def shards(
    request_owner, page_list, context_len, lin_state, decay_rate, lin_query, lin_keyval, soft_query, new_keyval,
    page_pool,
):
    tab = tables(request_owner, page_list, context_len, lax.axis_index("head"))
    vmem = pl.BlockSpec(memory_space=pltpu.VMEM)
    hbm = pl.BlockSpec(memory_space=pl.ANY)
    lin, soft = pl.pallas_call(
        kernel,
        out_shape=[jax.ShapeDtypeStruct((2, WIDTH, WIDTH), jnp.float32)] * 2,
        in_specs=[pl.BlockSpec(memory_space=pltpu.SMEM)] + [vmem] * 5 + [hbm] * 2,
        out_specs=[vmem] * 2,
        scratch_shapes=[
            pltpu.VMEM(lin_state.shape, jnp.float32),
            pltpu.VMEM(page_pool.shape, jnp.bfloat16),
            pltpu.VMEM((N, 2, WIDTH, WIDTH), jnp.bfloat16),
            pltpu.VMEM((N, 2, 2, 512), jnp.bfloat16),
            pltpu.VMEM((N, 2, 2, 2, 512), jnp.bfloat16),
            pltpu.VMEM((N, 2, 8, WIDTH), jnp.float32),
            pltpu.VMEM((N, 2, 8, WIDTH), jnp.float32),
            pltpu.VMEM((N, 2, 64, WIDTH), jnp.int32),
            pltpu.VMEM((N, 2, 64, WIDTH), jnp.int32),
            pltpu.VMEM((N, 8, WIDTH), jnp.float32),
            pltpu.VMEM((N, 8, WIDTH), jnp.float32),
            pltpu.VMEM((2, WIDTH, WIDTH), jnp.float32),
            pltpu.VMEM((2, 2, WIDTH, WIDTH), jnp.float32),
            pltpu.SemaphoreType.DMA((7,)),
            pltpu.SemaphoreType.DMA((6, N)),
            pltpu.SemaphoreType.DMA((6, N)),
        ],
        compiler_params=pltpu.CompilerParams(
            collective_id=0, has_side_effects=True, vmem_limit_bytes=56 * 1024 * 1024
        ),
    )(tab, decay_rate.reshape(1, 64), lin_query, lin_keyval, soft_query, new_keyval, lin_state, page_pool)
    return rows_last(lin), rows_last(soft)


def solution(mesh):
    return jax.shard_map(
        shards,
        mesh=mesh,
        in_specs=(
            P("grp"), P("grp", None), P("grp"), P("grp", "head", None, None), P(),
            P(("grp", "head"), None, None), P(("grp", "head"), None, None, None),
            P(("grp", "head"), None, None), P(("grp", "head"), None, None, None),
            P(("grp", "head"), None, None, None),
        ),
        out_specs=(P(("grp", "head"), None, None), P(("grp", "head"), None, None)),
        check_vma=False,
    )
```

time: 449 us -> 55.3 us (0.12)
  waiting for transfers between devices: 317 us -> 0 us
  local copies, waits for them, and re-layouts: 56.7 us -> 3.75 us
  Pallas kernels: 0 us -> 45 us
  other arithmetic: 35.7 us -> 4.85 us
  matrix products: 23.9 us -> 0 us
  starting transfers between devices: 14.1 us -> 0 us
    all_to_all x2 -> x0, waiting for transfers between devices: 317 us -> none  [the longest x1 219 us: shards(): lax.all_to_all(outgoing, 'head', split_axis=0, concat_axis=0, tiled=True)]
    pallas_call x0 -> x1, Pallas kernels: none -> 45 us  [shards(): pl.pallas_call(kernel, out_shape=[jax.ShapeDtypeStruct((2, WIDTH, WIDTH),...]
    gather x8 -> x0, local copies, waits for them, and re-layouts: 32 us -> none  [the longest x1 10.5 us: shards(): my_pages = jnp.take(arrived, my_position, axis=0)]
    select_n x10 -> x3, other arithmetic: 30.2 us -> 0.72 us  [the longest x1 0.69 us: tables(): local = (page_list % 16).reshape(-1)]
    dot_general x6 -> x0, matrix products: 23.9 us -> none  [the longest x2 15.2 us: lightning(): jnp.einsum('bhd,bhde->bhe', query_now, state, precision=lax.Precision.HIG...]
    slice x4 -> x0, local copies, waits for them, and re-layouts: 18.9 us -> none  [the longest x2 12.4 us: page_block(): page[0].reshape(page_size, kvh, width)]
    all_to_all x2 -> x0, starting transfers between devices: 14.1 us -> none  [the longest x1 8.31 us: shards(): lax.all_to_all(ordered, 'head', split_axis=0, concat_axis=1, tiled=True)]
  transfers between devices with their start and end apart: 2 -> 0, of which waited for: 2 -> 0; matrix products, arithmetic and copies ran while one was open for 11% -> 0% of each run, Pallas kernels for 0% -> 0%
where the time goes in v1:
time: 55.3 us; the launch traced here: 54.2 us
  Pallas kernels  45 us (81%)
  other arithmetic  4.85 us (9%)
  local copies, waits for them, and re-layouts  3.75 us (7%)
  between operations  0.67 us (1%)
    pallas_call x1, Pallas kernels, shards(): pl.pallas_call(kernel, out_shape=[jax.ShapeDtypeStruct((2, WIDTH, WIDTH),...  45 us
    unnamed x2, local copies, waits for them, and re-layouts  3.14 us

profile of v1, /device:TPU:0, one launch (start us, length us, event | category | flops | bytes accessed | tf_op | source)
XLA Modules:
  0.0 54.2 jit_solution(1363914926331439650)
XLA Ops:
  0.6 0.9 %select_reduce_fusion.3 = s32[32]{0:T(128)S(1)} fusion(s32[32]{0:T(128)} %param.10), kind=kLoop, calls=%fused_computation.6 | loop fusion | flops 5088 | bytes 256 | tf_op jit(solution)/shard_map/reduce_sum | solution.py:25
  1.5 0.7 %fusion.1 = pred[32,8]{0,1:T(8,128)(4,1)S(1)} fusion(s32[32,8]{0,1:T(8,128)} %param.11, s32[]{:T(128)S(6)} %axis_index.12), kind=kLoop, calls=%fused_computation.14 | loop fusion | flops 4096 | bytes 1284 | tf_op jit(solution)/shard_map/eq | solution.py:29
  2.3 0.7 %broadcast_multiply_fusion = (s32[32]{0:T(128)S(1)}, s32[32]{0:T(128)S(1)}) fusion(s32[32]{0:T(128)S(1)} %select_reduce_fusion.3, s32[32]{0:T(128)} %param.10), kind=kLoop, calls=%fused_computation.38 | loop fusion | flops 96 | bytes 512 | tf_op jit(solution)/shard_map/mul | solution.py:30
  2.9 0.1 select_reduce_fusion.2
  3.0 0.1 copy.19
  3.1 0.1 reshape.280
  3.2 0.7 %clamp_multiply_fusion = s32[32,8]{0,1:T(8,128)S(1)} fusion(s32[8]{0:T(128)S(1)} %iota_multiply_fusion, s32[32]{0:T(128)} %param.12), kind=kLoop, calls=%fused_computation.15 | loop fusion | flops 768 | bytes 1184 | tf_op jit(solution)/shard_map/mul | solution.py:36
  4.0 0.7 %add_select_fusion = s32[32,8]{0,1:T(8,128)S(1)} fusion(s32[32,8]{0,1:T(8,128)} %param.11), kind=kLoop, calls=%fused_computation.9 | loop fusion | flops 2816 | bytes 2048 | tf_op jit(solution)/shard_map/jit(remainder)/select_n | solution.py:33
  4.7 0.1 copy.20
  4.7 0.1 reshape.281
  4.8 0.1 copy.21
  4.9 0.1 mul.62
  5.0 0.1 iota_add_fusion
  5.1 0.1 add.129
  5.2 0.2 select_reduce_fusion
  5.4 0.1 select_reduce_fusion.1
  5.5 0.6 %pad_add_fusion.tab = s32[64]{0:T(128)} fusion(s32[32]{0:T(128)S(1)} %select_reduce_fusion.1, s32[32]{0:T(128)S(1)} %select_reduce_fusion.2), kind=kLoop, calls=%fused_computation.35 | loop fusion | flops 64 | bytes 512 | tf_op jit(solution)/shard_map/concatenate | solution.py:40
  6.1 45.0 %shard_map.113 = (f32[2,128,128]{2,1,0:T(8,128)}, f32[2,128,128]{2,1,0:T(8,128)}) custom-call(s32[64]{0:T(128)} %pad_add_fusion.tab, f32[1,64]{1,0:T(1,128)} %bitcast.13, bf16[2,2,8192]{2,1,0:T(2,128)(2,1)} %lq.1, bf16[2,2,2,8192]{3,2,1,0:T(2,128)(2,1)} %lkv.1, bf16[2,2,8192]{2,1,0:T(2,128)(2,1)} %sq.1, bf16[2,2,2,1024]{3,2,1,0:T(2,128)(2,1)} %nkv.1, ...), custom_call_target="tpu_custom_call" | custom-call | tf_op jit(solution)/shard_map/pallas_call | solution.py:335
  51.1 1.6 %copy.26 = f32[2,2,8192]{2,1,0:T(2,128)} copy(f32[2,2,8192]{2,1,0:T(2,128)} %bitcast.12) | data formatting | bytes 262144
  52.7 1.6 %copy.27 = f32[2,2,8192]{2,1,0:T(2,128)} copy(f32[2,2,8192]{2,1,0:T(2,128)} %bitcast.11) | data formatting | bytes 262144
  (3 shorter events, 0.0 us)

commit v2 on v1

v2 whole, which is shorter than its diff:
```python
import functools
import math

import jax
import jax.numpy as jnp
from jax import lax
from jax.experimental import pallas as pl
from jax.experimental.pallas import tpu as pltpu
from jax.sharding import PartitionSpec as P

MESH = pl.DeviceIdType.MESH
N = 16
WIDTH = 128
KVH = 8
CODES = 32000.0
LOW = -1e30
SCALE = 1.0 / math.sqrt(128.0)


def offsets(n):
    m = jnp.maximum(n - 7, 0)
    a = jnp.where(n < 4, n - 1, m // 3)
    b = jnp.where(n < 7, n - 4, m % 3)
    dz = jnp.where((n >= 1) & ((n < 4) | (n >= 7)), 1 + 2 * a - 3 * (a // 2), 0)
    dy = jnp.where(n >= 4, 1 + 2 * b - 3 * (b // 2), 0)
    return dz, dy


DIST = (1, 3, 2)
SLOT = {(0, 0): 0}
for _k, _d in enumerate(DIST):
    SLOT[_d, 0] = 1 + _k
    SLOT[0, _d] = 4 + _k
    for _l, _e in enumerate(DIST):
        SLOT[_d, _e] = 7 + 3 * _k + _l


def make_tables(owner, pages, length, me):
    sub = lax.broadcasted_iota(jnp.int32, (32, 32), 0)
    lane = lax.broadcasted_iota(jnp.int32, (32, 32), 1)

    def column(row):
        return jnp.sum(jnp.where(sub == lane, row, 0), axis=1, keepdims=True)

    slot = jnp.sum(jnp.where((column(owner) == owner) & (sub < lane), 1, 0), axis=0, keepdims=True)
    row = owner * 2 + slot
    request_of = jnp.sum(jnp.where(column(row) == lane, sub, 0), axis=0, keepdims=True)
    j = lax.broadcasted_iota(jnp.int32, (8, 32), 0)
    count = jnp.clip(length - j * WIDTH, 0, WIDTH)
    here = (lax.shift_right_logical(pages, 4) == me) & (count > 0)
    code = (pages & 15) + count * 16
    least = jnp.min(jnp.where(here, j, 8), axis=0, keepdims=True)
    most = jnp.max(jnp.where(here, j, -1), axis=0, keepdims=True)
    first = jnp.sum(jnp.where(here & (j == least), code, 0), axis=0, keepdims=True)
    second = jnp.sum(jnp.where(here & (j == most) & (most != least), code, 0), axis=0, keepdims=True)
    return request_of, first, second


def kernel(
    owner, pages, length, rate, sq, nkv, lq, lkv, state_hbm, pool_hbm, lin_ref, soft_ref,
    state, pool, q_all, lq_mid, lkv_mid, lq_in, lkv_in, lin_send, lin_in, res_send, res_in, meta_send, meta_in,
    run_acc, run_meta, tab_rows, tab, local_sem, half_send, half_recv, mid_send, mid_recv, back_send, back_recv,
):
    me = lax.axis_index("head")
    mz, my = me // 4, me % 4

    def at_offset(dz, dy):
        return (mz + dz) % 4 * 4 + (my + dy) % 4

    def behind(n):
        dz, dy = offsets(n)
        return at_offset(4 - dz, 4 - dy)

    def remote(src, dst, send, recv, to):
        return pltpu.make_async_remote_copy(
            src_ref=src, dst_ref=dst, send_sem=send, recv_sem=recv, device_id={"head": to}, device_id_type=MESH
        )

    def half(h, src, dst, to):
        part = pl.ds(64 * h, 64)
        return remote(
            q_all.at[src, :, part], q_all.at[dst, :, part], half_send.at[h, dst], half_recv.at[h, dst], to
        )

    def lin_back(n):
        mine = pl.ds(pl.multiple_of(me * 8, 8), 8)
        return remote(lin_send.at[n], lin_in.at[:, mine], back_send.at[0, n], back_recv.at[0, n], behind(n))

    def back(n):
        to = behind(n)
        return (
            remote(res_send.at[n], res_in.at[n], back_send.at[1, n], back_recv.at[1, n], to),
            remote(meta_send.at[n], meta_in.at[n], back_send.at[2, n], back_recv.at[2, n], to),
        )

    barrier = pltpu.get_barrier_semaphore()
    for d in DIST:
        for to in (at_offset(d, 0), at_offset(0, d)):
            pl.semaphore_signal(barrier, inc=1, device_id={"head": to}, device_id_type=MESH)
    fetch_state = pltpu.make_async_copy(state_hbm, state, local_sem.at[0])
    fetch_pool = pltpu.make_async_copy(pool_hbm, pool, local_sem.at[1])
    fetch_state.start()
    fetch_pool.start()

    def wide(dz):
        return pl.ds(pl.multiple_of((mz + dz) % 4 * 2048, 2048), 2048)

    def narrow(dy):
        return pl.ds(pl.multiple_of((my + dy) % 4 * 512, 512), 512)

    own_mid = [
        pltpu.make_async_copy(lq.at[:, :, wide(0)], lq_mid.at[0], local_sem.at[2]),
        pltpu.make_async_copy(lkv.at[:, :, :, wide(0)], lkv_mid.at[0], local_sem.at[3]),
    ]
    for copy in own_mid:
        copy.start()
    for r in range(2):
        q_all[0, r] = sq[r].astype(jnp.float32).T.astype(jnp.bfloat16)
    tab_rows[...] = jnp.zeros((8, WIDTH), jnp.int32)
    for n, row in enumerate(make_tables(owner[...], pages[...], length[...], me)):
        tab_rows[n:n + 1, 0:32] = row
    fill_tab = pltpu.make_async_copy(tab_rows, tab, local_sem.at[4])
    fill_tab.start()
    pl.semaphore_wait(barrier, 6)

    mids = []
    for k, d in enumerate(DIST):
        to = at_offset(d, 0)
        mids.append(remote(lq.at[:, :, wide(d)], lq_mid.at[d], mid_send.at[0, d], mid_recv.at[0, d], to))
        mids.append(remote(lkv.at[:, :, :, wide(d)], lkv_mid.at[d], mid_send.at[1, d], mid_recv.at[1, d], to))
    for copy in mids:
        copy.start()

    first = {}
    for d in DIST:
        first[0, d] = half(0, 0, SLOT[d, 0], at_offset(d, 0))
        first[1, d] = half(1, 0, SLOT[0, d], at_offset(0, d))
    for copy in first.values():
        copy.start()
    for d in DIST:
        half(0, 0, SLOT[0, d], at_offset(0, d)).start()
        half(1, 0, SLOT[d, 0], at_offset(d, 0)).start()
    for copy in own_mid:
        copy.wait()
    for d in DIST:
        first[0, d].wait_recv()
        for e in DIST:
            half(0, SLOT[d, 0], SLOT[d, e], at_offset(0, e)).start()
        first[1, d].wait_recv()
        for e in DIST:
            half(1, SLOT[0, d], SLOT[e, d], at_offset(e, 0)).start()
    for copy in mids:
        copy.wait_recv()
    lasts = []
    for d in DIST:
        to = at_offset(0, d)
        lasts.append(remote(lq_mid.at[:, :, :, narrow(d)], lq_in.at[d], mid_send.at[2, d], mid_recv.at[2, d], to))
        lasts.append(remote(lkv_mid.at[:, :, :, :, narrow(d)], lkv_in.at[d], mid_send.at[3, d], mid_recv.at[3, d], to))
    for copy in lasts:
        copy.start()
    own_last = [
        pltpu.make_async_copy(lq_mid.at[:, :, :, narrow(0)], lq_in.at[0], local_sem.at[2]),
        pltpu.make_async_copy(lkv_mid.at[:, :, :, :, narrow(0)], lkv_in.at[0], local_sem.at[3]),
    ]
    for copy in own_last:
        copy.start()

    row8 = lax.broadcasted_iota(jnp.int32, (8, 64), 0)
    lane8 = lax.broadcasted_iota(jnp.int32, (8, 64), 1)
    rates = jnp.sum(jnp.where(lane8 == me * 4 + row8 // 2, rate[...], 0.0), axis=1, keepdims=True)
    second = lax.broadcasted_iota(jnp.int32, (8, 1), 0) % 2 == 1
    lam = jnp.exp(-rates)
    lam_state = jnp.where(second, lam * lam, lam)
    lam_first = jnp.where(second, lam, 1.0)
    lam_second = jnp.where(second, 1.0, 0.0)
    head_of = lax.broadcasted_iota(jnp.int32, (8, WIDTH), 0) // 2

    def spread(x):
        return jnp.concatenate(
            [jnp.broadcast_to(x[:, h * WIDTH:(h + 1) * WIDTH], (2, WIDTH)) for h in range(4)], axis=0
        )

    def lightning(n):
        dz, dy = offsets(n)
        owner_at = behind(n)
        for r in range(2):
            request = tab[0, owner_at * 2 + r] & 31
            q = lq_in[dy, dz, r].astype(jnp.float32)
            q = jnp.concatenate([q[:, h * WIDTH:(h + 1) * WIDTH] for h in range(4)], axis=0)
            kv1 = lkv_in[dy, dz, r, 0].astype(jnp.float32)
            kv2 = lkv_in[dy, dz, r, 1].astype(jnp.float32)
            q_bf = q.astype(jnp.bfloat16)
            q_two = jnp.concatenate([q_bf, q_bf], axis=1)
            y = jnp.zeros((8, WIDTH), jnp.float32)
            for h in range(4):
                s = state[request, h]
                high = s.astype(jnp.bfloat16)
                low = (s - high.astype(jnp.float32)).astype(jnp.bfloat16)
                got = jnp.dot(q_two, jnp.concatenate([high, low], axis=0), preferred_element_type=jnp.float32)
                y = jnp.where(head_of == h, got, y)
            k1, v1, k2, v2 = spread(kv1[0:1]), spread(kv1[1:2]), spread(kv2[0:1]), spread(kv2[1:2])
            qk1 = jnp.sum(q * k1, axis=1, keepdims=True)
            qk2 = jnp.sum(q * k2, axis=1, keepdims=True)
            y = lam_state * y + (lam_first * qk1) * v1 + (lam_second * qk2) * v2
            norm = jnp.sqrt(jnp.mean(y * y, axis=1, keepdims=True) + 1e-5)
            lin_send[n, r] = y / norm

    position = lax.broadcasted_iota(jnp.int32, (WIDTH, WIDTH), 0)
    lane_head = lax.broadcasted_iota(jnp.int32, (WIDTH, WIDTH), 1) // 16
    of_head = [jnp.where(lane_head == c, 1.0, 0.0).astype(jnp.bfloat16) for c in range(KVH)]

    def page_part(page, count, q):
        scores = sum(
            jnp.dot(
                pool[page, 0, :, c * WIDTH:(c + 1) * WIDTH], q * of_head[c], preferred_element_type=jnp.float32
            )
            for c in range(KVH)
        ) * SCALE
        live = position < count
        top = jnp.max(jnp.where(live, scores, LOW), axis=0, keepdims=True)
        weight = jnp.where(live, jnp.exp(scores - top), 0.0)
        total = jnp.sum(weight, axis=0, keepdims=True)
        rounded = weight.astype(jnp.bfloat16)
        acc = sum(
            lax.dot_general(
                pool[page, 1, :, c * WIDTH:(c + 1) * WIDTH], rounded * of_head[c], (((0,), (0,)), ((), ())),
                preferred_element_type=jnp.float32,
            )
            for c in range(KVH)
        )
        return top, total, acc

    def softmax(n):
        owner_at = behind(n)
        a, b = tab[0, owner_at * 2] & 31, tab[0, owner_at * 2 + 1] & 31
        first_a, second_a, first_b, second_b = tab[1, a], tab[2, a], tab[1, b], tab[2, b]
        codes = (
            jnp.where(first_a > 0, first_a, first_b),
            jnp.where(second_a > 0, second_a, jnp.where(first_a > 0, first_b, second_b)),
        )
        rows = (jnp.where(first_a > 0, 0, 1), jnp.where(second_a > 0, 0, 1))
        found = []
        for code, row in zip(codes, rows):
            q = jnp.where(row == 1, q_all[n, 1], q_all[n, 0])
            found.append((row, *page_part(code & 15, lax.shift_right_logical(code, 4), q)))
        metas = []
        for r in range(2):
            tops = [jnp.where(row == r, top, LOW) for row, top, _, _ in found]
            peak = jnp.maximum(tops[0], tops[1])
            factors = [jnp.where(row == r, jnp.exp(t - peak), 0.0) for t, (row, _, _, _) in zip(tops, found)]
            total = factors[0] * found[0][2] + factors[1] * found[1][2]
            acc = factors[0] * found[0][3] + factors[1] * found[1][3]
            most = jnp.maximum(jnp.max(jnp.abs(acc), axis=0, keepdims=True), 1e-30)
            coded = (acc * (CODES / most) + 32768.5).astype(jnp.int32)
            res_send[n, r] = lax.shift_left(coded[:64], 16) | coded[64:]
            metas += [peak, total, most * (1.0 / CODES)]
        meta_send[n] = jnp.concatenate(metas + [jnp.zeros((2, WIDTH), jnp.float32)], axis=0)

    fetch_pool.wait()
    fill_tab.wait()
    def lightning_pair(p, carry):
        for n in (2 * p, 2 * p + 1):
            lightning(n)
        for n in (2 * p, 2 * p + 1):

            @pl.when(n > 0)
            def _(n=n):
                lin_back(n).start()

        return carry

    def pair(p, carry):
        @pl.when(p == 4)
        def _():
            for copy in own_last:
                copy.wait()
            for copy in lasts:
                copy.wait_recv()
            fetch_state.wait()
            lax.fori_loop(0, 8, lightning_pair, 0)

        for n in (2 * p, 2 * p + 1):

            @pl.when(n >= 4)
            def _(n=n):
                half(0, 0, n, at_offset(1, 0)).wait_recv()

            @pl.when((n >= 7) | ((n >= 1) & (n < 4)))
            def _(n=n):
                half(1, 0, n, at_offset(1, 0)).wait_recv()

        for n in (2 * p, 2 * p + 1):
            softmax(n)
        for n in (2 * p, 2 * p + 1):

            @pl.when(n > 0)
            def _(n=n):
                for copy in back(n):
                    copy.start()

        return carry

    lax.fori_loop(0, 8, pair, 0)
    keep = pltpu.make_async_copy(
        lin_send.at[0], lin_in.at[:, pl.ds(pl.multiple_of(me * 8, 8), 8)], local_sem.at[5]
    )
    keep.start()

    step = lax.broadcasted_iota(jnp.int32, (1, WIDTH), 1) % 2

    def by_head(x):
        return jnp.concatenate(
            [jnp.broadcast_to(x[:, c * WIDTH:(c + 1) * WIDTH], (16, WIDTH)) for c in range(KVH)], axis=0
        ).T

    def merge_in(acc, peak_old, total, r, sources):
        peak = peak_old
        for meta, _ in sources:
            peak = jnp.maximum(peak, meta[3 * r:3 * r + 1])
        keep_factor = jnp.exp(peak_old - peak)
        total = total * keep_factor
        factors = []
        shift = jnp.zeros((1, WIDTH), jnp.float32)
        for meta, _ in sources:
            factor = jnp.exp(meta[3 * r:3 * r + 1] - peak)
            total = total + factor * meta[3 * r + 1:3 * r + 2]
            factors.append(factor * meta[3 * r + 2:3 * r + 3])
            shift = shift + factors[-1] * 32768.0
        upper = acc[:64] * keep_factor - shift
        lower = acc[64:] * keep_factor - shift
        for factor, (_, words) in zip(factors, sources):
            upper = upper + factor * lax.shift_right_logical(words, 16).astype(jnp.float32)
            lower = lower + factor * (words & 65535).astype(jnp.float32)
        return jnp.concatenate([upper, lower], axis=0), peak, total

    def keep_run(r, acc, peak, total):
        run_acc[r] = acc
        run_meta[r, 0:1] = peak
        run_meta[r, 1:2] = total

    for r in range(2):
        q = q_all[0, r].astype(jnp.float32)
        kv = [nkv[r, t].astype(jnp.float32) for t in range(2)]
        s0 = jnp.sum(q * by_head(kv[0][0:1]), axis=0, keepdims=True) * SCALE
        s1 = jnp.sum(q * by_head(kv[1][0:1]), axis=0, keepdims=True) * SCALE
        top = jnp.where(step == 1, jnp.maximum(s0, s1), s0)
        w0 = jnp.exp(s0 - top)
        w1 = jnp.where(step == 1, jnp.exp(s1 - top), 0.0)
        r0 = w0.astype(jnp.bfloat16).astype(jnp.float32)
        r1 = w1.astype(jnp.bfloat16).astype(jnp.float32)
        acc = r0 * by_head(kv[0][1:2]) + r1 * by_head(kv[1][1:2])
        keep_run(r, *merge_in(acc, top, w0 + w1, r, [(meta_send[0], res_send[0, r])]))

    def merge(p, carry):
        slots = [3 * p + 1 + k for k in range(3)]
        for n in slots:
            for copy in back(n):
                copy.wait_recv()
        for r in range(2):
            sources = [(meta_in[n], res_in[n, r]) for n in slots]
            keep_run(r, *merge_in(run_acc[r], run_meta[r, 0:1], run_meta[r, 1:2], r, sources))
        return carry

    lax.fori_loop(0, 5, merge, 0)
    for r in range(2):
        soft_ref[r] = (run_acc[r] / run_meta[r, 1:2]).T

    def finish(n, carry):
        half(0, 0, n, at_offset(1, 0)).wait_send()
        half(1, 0, n, at_offset(1, 0)).wait_send()
        lin = lin_back(n)
        lin.wait_recv()
        lin.wait_send()
        for copy in back(n):
            copy.wait_send()
        return carry

    lax.fori_loop(1, N, finish, 0)
    for copy in mids + lasts:
        copy.wait_send()
    keep.wait()
    lin_ref[...] = lin_in[...]


def copy_kernel(a_ref, b_ref, c_ref, d_ref):
    c_ref[...] = a_ref[...]
    d_ref[...] = b_ref[...]


def rows_first(x):
    return x.reshape(2, 2, 64, WIDTH).transpose(0, 2, 1, 3).reshape(2, WIDTH, WIDTH)


def rows_last(x):
    return x.reshape(2, 64, 2, WIDTH).transpose(0, 2, 1, 3).reshape(2, 2, 64 * WIDTH)


def shards(
    request_owner, page_list, context_len, lin_state, decay_rate, lin_query, lin_keyval, soft_query, new_keyval,
    page_pool,
):
    vmem = pl.BlockSpec(memory_space=pltpu.VMEM)
    hbm = pl.BlockSpec(memory_space=pl.ANY)
    out = [jax.ShapeDtypeStruct((2, WIDTH, WIDTH), jnp.float32)] * 2
    lin, soft = pl.pallas_call(
        kernel,
        out_shape=out,
        in_specs=[vmem] * 6 + [hbm] * 4,
        out_specs=[vmem] * 2,
        scratch_shapes=[
            pltpu.VMEM(lin_state.shape, jnp.float32),
            pltpu.VMEM(page_pool.shape, jnp.bfloat16),
            pltpu.VMEM((N, 2, WIDTH, WIDTH), jnp.bfloat16),
            pltpu.VMEM((4, 2, 2, 2048), jnp.bfloat16),
            pltpu.VMEM((4, 2, 2, 2, 2048), jnp.bfloat16),
            pltpu.VMEM((4, 4, 2, 2, 512), jnp.bfloat16),
            pltpu.VMEM((4, 4, 2, 2, 2, 512), jnp.bfloat16),
            pltpu.VMEM((N, 2, 8, WIDTH), jnp.float32),
            pltpu.VMEM((2, WIDTH, WIDTH), jnp.float32),
            pltpu.VMEM((N, 2, 64, WIDTH), jnp.int32),
            pltpu.VMEM((N, 2, 64, WIDTH), jnp.int32),
            pltpu.VMEM((N, 8, WIDTH), jnp.float32),
            pltpu.VMEM((N, 8, WIDTH), jnp.float32),
            pltpu.VMEM((2, WIDTH, WIDTH), jnp.float32),
            pltpu.VMEM((2, 8, WIDTH), jnp.float32),
            pltpu.VMEM((8, WIDTH), jnp.int32),
            pltpu.SMEM((8, WIDTH), jnp.int32),
            pltpu.SemaphoreType.DMA((6,)),
            pltpu.SemaphoreType.DMA((2, N)),
            pltpu.SemaphoreType.DMA((2, N)),
            pltpu.SemaphoreType.DMA((4, 4)),
            pltpu.SemaphoreType.DMA((4, 4)),
            pltpu.SemaphoreType.DMA((3, N)),
            pltpu.SemaphoreType.DMA((3, N)),
        ],
        compiler_params=pltpu.CompilerParams(
            collective_id=0, has_side_effects=True, vmem_limit_bytes=56 * 1024 * 1024
        ),
    )(
        request_owner.reshape(1, 32), page_list.T, context_len.reshape(1, 32), decay_rate.reshape(1, 64),
        rows_first(soft_query), new_keyval, lin_query, lin_keyval, lin_state, page_pool,
    )
    lin, soft = pl.pallas_call(copy_kernel, out_shape=out, in_specs=[vmem] * 2, out_specs=[vmem] * 2)(lin, soft)
    return rows_last(lin), rows_last(soft)


def solution(mesh):
    return jax.shard_map(
        shards,
        mesh=mesh,
        in_specs=(
            P("grp"), P("grp", None), P("grp"), P("grp", "head", None, None), P(),
            P(("grp", "head"), None, None), P(("grp", "head"), None, None, None),
            P(("grp", "head"), None, None), P(("grp", "head"), None, None, None),
            P(("grp", "head"), None, None, None),
        ),
        out_specs=(P(("grp", "head"), None, None), P(("grp", "head"), None, None)),
        check_vma=False,
    )
```

time: 55.3 us -> 40.2 us (0.73); the launches traced: 54.2 us -> 40 us
  Pallas kernels: 45 us -> 39.3 us
  other arithmetic: 4.85 us -> 0 us
  local copies, waits for them, and re-layouts: 3.75 us -> 0 us
    pallas_call x1 -> x2, Pallas kernels: 45 us -> 39.3 us  [the longest x1 37.7 us: shards(): pl.pallas_call(kernel, out_shape=out, in_specs=[vmem] * 6 + [hbm] * 4, ou...]
    unnamed x2 -> x0, local copies, waits for them, and re-layouts: 3.14 us -> none
    mul x3 -> x0, other arithmetic: 1.4 us -> none  [the longest x1 0.73 us: tables(): packed = local + entry // 8 % 2 * 16 + count * 32]
    reduce_sum x4 -> x0, other arithmetic: 1.36 us -> none  [the longest x1 0.91 us: tables(): slots = jnp.sum(jnp.where(same & earlier, 1, 0), axis=1).astype(jnp.int32)]
    select_n x3 -> x0, other arithmetic: 0.72 us -> none  [the longest x1 0.69 us: tables(): local = (page_list % 16).reshape(-1)]
    eq x1 -> x0, other arithmetic: 0.7 us -> none  [tables(): here = page_list // 16 == me]
    concatenate x1 -> x0, other arithmetic: 0.59 us -> none  [tables(): return jnp.concatenate([request_of, slot_codes]).astype(jnp.int32)]
where the time goes in v2:
time: 40.2 us; the launch traced here: 40 us
  Pallas kernels  39.3 us (98%)
  between operations  0.64 us (2%)
    pallas_call x1, Pallas kernels, shards(): pl.pallas_call(kernel, out_shape=out, in_specs=[vmem] * 6 + [hbm] * 4, ou...  37.7 us
    pallas_call x1, Pallas kernels, shards(): pl.pallas_call(copy_kernel, out_shape=out, in_specs=[vmem] * 2, out_specs...  1.68 us

profile of v2, /device:TPU:0, one launch (start us, length us, event | category | flops | bytes accessed | tf_op | source)
XLA Modules:
  0.0 40.0 jit_solution(10949514985956119672)
XLA Ops:
  0.6 37.7 %shard_map.113 = (f32[2,128,128]{2,1,0:T(8,128)}, f32[2,128,128]{2,1,0:T(8,128)}) custom-call(s32[1,32]{1,0:T(1,128)} %bitcast.21, s32[8,32]{1,0:T(8,128)} %bitcast.20, s32[1,32]{1,0:T(1,128)} %bitcast.22, f32[1,64]{1,0:T(1,128)} %bitcast.23, bf16[2,128,128]{2,1,0:T(8,128)(2,1)} %bitcast.19, bf16[2,2,2,1024]{3,2,1,0:T(2,128)(2,1)} %nkv.1, ...), custom_call_target="tpu_custom_call" | custom-call | tf_op jit(solution)/shard_map/pallas_call | solution.py:405
  38.3 1.7 %shard_map.114 = (f32[2,128,128]{2,1,0:T(8,128)}, f32[2,128,128]{2,1,0:T(8,128)}) custom-call(f32[2,128,128]{2,1,0:T(8,128)} %get-tuple-element.6.a_ref, f32[2,128,128]{2,1,0:T(8,128)} %get-tuple-element.7.b_ref), custom_call_target="tpu_custom_call" | custom-call | tf_op jit(solution)/shard_map/pallas_call | solution.py:443

commit v3 on v2

v3 whole, which is shorter than its diff:
```python
import functools
import math

import jax
import jax.numpy as jnp
from jax import lax
from jax.experimental import pallas as pl
from jax.experimental.pallas import tpu as pltpu
from jax.sharding import PartitionSpec as P

MESH = pl.DeviceIdType.MESH
N = 16
WIDTH = 128
KVH = 8
CODES = 32000.0
LOW = -1e30
NONE = -505.0
LEVEL_UNIT = 2.0**22
SIZE_UNIT = 2.0**16
SCALE = 1.0 / math.sqrt(128.0)


DIST = (1, 3, 2)
OFFSETS = ((0, 0), (1, 0), (0, 1), (3, 0), (0, 3), (2, 0), (0, 2), (1, 1), (1, 3), (3, 1), (3, 3), (1, 2), (2, 1), (3, 2), (2, 3), (2, 2))
SLOT = {offset: n for n, offset in enumerate(OFFSETS)}


def offsets(n):
    return tuple(
        sum(jnp.where(n == i, offset[axis], 0) for i, offset in enumerate(OFFSETS) if offset[axis]) for axis in (0, 1)
    )


def make_tables(owner, pages, length, me):
    sub = lax.broadcasted_iota(jnp.int32, (32, 32), 0)
    lane = lax.broadcasted_iota(jnp.int32, (32, 32), 1)

    def column(row):
        return jnp.sum(jnp.where(sub == lane, row, 0), axis=1, keepdims=True)

    slot = jnp.sum(jnp.where((column(owner) == owner) & (sub < lane), 1, 0), axis=0, keepdims=True)
    row = owner * 2 + slot
    request_of = jnp.sum(jnp.where(column(row) == lane, sub, 0), axis=0, keepdims=True)
    j = lax.broadcasted_iota(jnp.int32, (8, 32), 0)
    count = jnp.clip(length - j * WIDTH, 0, WIDTH)
    here = (lax.shift_right_logical(pages, 4) == me) & (count > 0)
    code = (pages & 15) + count * 16
    least = jnp.min(jnp.where(here, j, 8), axis=0, keepdims=True)
    most = jnp.max(jnp.where(here, j, -1), axis=0, keepdims=True)
    first = jnp.sum(jnp.where(here & (j == least), code, 0), axis=0, keepdims=True)
    second = jnp.sum(jnp.where(here & (j == most) & (most != least), code, 0), axis=0, keepdims=True)
    return request_of, first, second


def kernel(
    owner, pages, length, rate, sq_hbm, nkv_hbm, lq_hbm, lkv_hbm, state_hbm, pool_hbm, lin_ref, soft_ref,
    state, pool, sq, nkv, lq, lkv, lin_fresh, lin_out, q_all, lin_pack, lin_mid, lin_all, lin_send, lin_in, part_send, part_in, mid_send, mid_in,
    tab_rows, tab, local_sem, half_send, half_recv, mid_sems, mid_recvs, back_send, back_recv,
    part_sems, part_recvs, last_sems, last_recvs,
):
    me = lax.axis_index("head")
    mz, my = me // 4, me % 4

    def at_offset(dz, dy):
        return (mz + dz) % 4 * 4 + (my + dy) % 4

    def behind(n):
        dz, dy = offsets(n)
        return at_offset(4 - dz, 4 - dy)

    def remote(src, dst, send, recv, to):
        return pltpu.make_async_remote_copy(
            src_ref=src, dst_ref=dst, send_sem=send, recv_sem=recv, device_id={"head": to}, device_id_type=MESH
        )

    def half(h, src, dst, to):
        rows = pl.ds(64 * h, 64)
        return remote(
            q_all.at[src, :, rows], q_all.at[dst, :, rows], half_send.at[h, dst], half_recv.at[h, dst], to
        )

    def lin_back(n):
        return remote(lin_send.at[n], lin_in.at[n], back_send.at[n], back_recv.at[n], behind(n))

    def part(h, dz, dy):
        to = at_offset(4 - dz, 0) if h == 0 else at_offset(0, 4 - dy)
        n = dz * 4 + dy
        return remote(part_send.at[h, n], part_in.at[h, n], part_sems.at[h, n], part_recvs.at[h, n], to)

    def last(h, d):
        to = at_offset(0, 4 - d) if h == 0 else at_offset(4 - d, 0)
        return remote(mid_send.at[h, d], mid_in.at[h, d], last_sems.at[h, d], last_recvs.at[h, d], to)

    barrier = pltpu.get_barrier_semaphore()
    for d in DIST:
        for to in (at_offset(d, 0), at_offset(0, d)):
            pl.semaphore_signal(barrier, inc=1, device_id={"head": to}, device_id_type=MESH)
    loads = [
        pltpu.make_async_copy(src, dst, local_sem.at[5 + n])
        for n, (src, dst) in enumerate(((sq_hbm, sq), (lq_hbm, lq), (lkv_hbm, lkv), (nkv_hbm, nkv)))
    ]
    for copy in loads:
        copy.start()
    fetch_pool = pltpu.make_async_copy(pool_hbm, pool, local_sem.at[1])
    fetch_state = pltpu.make_async_copy(state_hbm, state, local_sem.at[0])
    fetch_pool.start()
    fetch_state.start()
    tab_rows[...] = jnp.zeros((8, WIDTH), jnp.int32)
    for n, row in enumerate(make_tables(owner[...], pages[...], length[...], me)):
        tab_rows[n:n + 1, 0:32] = row
    fill_tab = pltpu.make_async_copy(tab_rows, tab, local_sem.at[4])
    fill_tab.start()
    for copy in loads:
        copy.wait()
    wide = [lq[r].astype(jnp.float32) for r in range(2)]
    for peer in range(N):
        lin_pack[peer // 4, peer % 4] = jnp.concatenate(
            [x[peer * 8:peer * 8 + 8] for x in wide], axis=0
        ).astype(jnp.bfloat16)
    own_mid = pltpu.make_async_copy(lin_pack.at[mz], lin_mid.at[0], local_sem.at[2])
    own_mid.start()
    for r in range(2):
        q_all[0, r] = sq[r].astype(jnp.float32).T.astype(jnp.bfloat16)

    row_of = lax.broadcasted_iota(jnp.int32, (WIDTH, 64), 0)
    lane_of = lax.broadcasted_iota(jnp.int32, (WIDTH, 64), 1)
    rates = jnp.sum(jnp.where(lane_of == row_of // 2, rate[...], 0.0), axis=1, keepdims=True)
    second = lax.broadcasted_iota(jnp.int32, (WIDTH, 1), 0) % 2 == 1
    lam = jnp.exp(-rates)
    lam_state = jnp.where(second, lam * lam, lam)
    lam_first = jnp.where(second, lam, 1.0)
    lam_second = jnp.where(second, 1.0, 0.0)
    odd = lax.broadcasted_iota(jnp.int32, (WIDTH, WIDTH), 0) % 2 == 1

    def keys_values(x):
        return jnp.where(odd, pltpu.roll(x, 1, 0), x), jnp.where(odd, x, pltpu.roll(x, WIDTH - 1, 0))

    for r in range(2):
        k1, v1 = keys_values(lkv[r, 0].astype(jnp.float32))
        k2, v2 = keys_values(lkv[r, 1].astype(jnp.float32))
        qk1 = jnp.sum(wide[r] * k1, axis=1, keepdims=True)
        qk2 = jnp.sum(wide[r] * k2, axis=1, keepdims=True)
        lin_fresh[r] = (lam_first * qk1) * v1 + (lam_second * qk2) * v2
    lin_fresh[2] = jnp.broadcast_to(lam_state, (WIDTH, WIDTH))
    pl.semaphore_wait(barrier, 6)

    mids = [
        remote(lin_pack.at[(mz + d) % 4], lin_mid.at[d], mid_sems.at[0, d], mid_recvs.at[0, d], at_offset(d, 0))
        for d in DIST
    ]
    for copy in mids:
        copy.start()

    first = {}
    for d in DIST:
        first[0, d] = half(0, 0, SLOT[d, 0], at_offset(d, 0))
        first[1, d] = half(1, 0, SLOT[0, d], at_offset(0, d))
    for copy in first.values():
        copy.start()
    for d in DIST:
        half(0, 0, SLOT[0, d], at_offset(0, d)).start()
        half(1, 0, SLOT[d, 0], at_offset(d, 0)).start()
    own_mid.wait()
    for copy in mids:
        copy.wait_recv()
    lasts = [
        remote(
            lin_mid.at[:, (my + d) % 4], lin_all.at[d], mid_sems.at[1, d], mid_recvs.at[1, d], at_offset(0, d)
        )
        for d in DIST
    ]
    for copy in lasts:
        copy.start()
    own_last = pltpu.make_async_copy(lin_mid.at[:, my], lin_all.at[0], local_sem.at[3])
    own_last.start()
    for d in DIST:
        first[0, d].wait_recv()
        for e in DIST:
            half(0, SLOT[d, 0], SLOT[d, e], at_offset(0, e)).start()
        first[1, d].wait_recv()
        for e in DIST:
            half(1, SLOT[0, d], SLOT[e, d], at_offset(e, 0)).start()

    head_of = lax.broadcasted_iota(jnp.int32, (8, WIDTH), 0) // 2

    def lightning(n):
        dz, dy = offsets(n)
        owner_at = behind(n)
        block = lin_all[dy, dz].astype(jnp.float32)
        for r in range(2):
            request = tab[0, owner_at * 2 + r] & 31
            q = block[8 * r:8 * r + 8].astype(jnp.bfloat16)
            q_two = jnp.concatenate([q, q], axis=1)
            y = jnp.zeros((8, WIDTH), jnp.float32)
            for h in range(4):
                s = state[request, h]
                high = s.astype(jnp.bfloat16)
                low = (s - high.astype(jnp.float32)).astype(jnp.bfloat16)
                got = jnp.dot(q_two, jnp.concatenate([high, low], axis=0), preferred_element_type=jnp.float32)
                y = jnp.where(head_of == h, got, y)
            lin_send[n, r] = y

    position = lax.broadcasted_iota(jnp.int32, (WIDTH, WIDTH), 0)
    lane_head = lax.broadcasted_iota(jnp.int32, (WIDTH, WIDTH), 1) // 16
    of_head = [jnp.where(lane_head == c, 1.0, 0.0).astype(jnp.bfloat16) for c in range(KVH)]

    def page_part(page, count, q):
        scores = sum(
            jnp.dot(
                pool[page, 0, :, c * WIDTH:(c + 1) * WIDTH], q * of_head[c], preferred_element_type=jnp.float32
            )
            for c in range(KVH)
        ) * SCALE
        live = position < count
        top = jnp.max(jnp.where(live, scores, LOW), axis=0, keepdims=True)
        weight = jnp.where(live, jnp.exp(scores - top), 0.0)
        total = jnp.sum(weight, axis=0, keepdims=True)
        rounded = weight.astype(jnp.bfloat16)
        acc = sum(
            lax.dot_general(
                pool[page, 1, :, c * WIDTH:(c + 1) * WIDTH], rounded * of_head[c], (((0,), (0,)), ((), ())),
                preferred_element_type=jnp.float32,
            )
            for c in range(KVH)
        )
        return top, total, acc

    def encode(found):
        words, logs = [], []
        for upper, lower, level in found:
            most = jnp.maximum(
                jnp.max(jnp.abs(upper), axis=0, keepdims=True), jnp.max(jnp.abs(lower), axis=0, keepdims=True)
            )
            size = jnp.ceil(jnp.log(jnp.maximum(most, 1e-30)) * SIZE_UNIT)
            inverse = CODES * jnp.exp(size * (-1.0 / SIZE_UNIT))
            high = (upper * inverse + 32768.5).astype(jnp.int32)
            low = (lower * inverse + 32768.5).astype(jnp.int32)
            words.append(lax.shift_left(high, 16) | low)
            logs += [(level * LEVEL_UNIT).astype(jnp.int32), size.astype(jnp.int32)]
        return jnp.concatenate(words + logs + [jnp.zeros((4, WIDTH), jnp.int32)], axis=0)

    def merged(sources, r, more=None):
        levels = [x[64 + 2 * r:65 + 2 * r].astype(jnp.float32) * (1.0 / LEVEL_UNIT) for x in sources]
        sizes = [x[65 + 2 * r:66 + 2 * r].astype(jnp.float32) * (1.0 / SIZE_UNIT) for x in sources]
        peak = functools.reduce(jnp.maximum, levels + ([more[2]] if more else []))
        weights = [jnp.where(x > NONE + 20.0, jnp.exp(x - peak), 0.0) for x in levels]
        total = sum(weights)
        factors = [w * jnp.exp(size) * (1.0 / CODES) for w, size in zip(weights, sizes)]
        shift = sum(factors) * 32768.0
        upper, lower = -shift, -shift
        if more:
            weight = jnp.exp(more[2] - peak)
            total = total + weight
            upper, lower = weight * more[0] - shift, weight * more[1] - shift
        for factor, x in zip(factors, sources):
            words = x[32 * r:32 * r + 32]
            upper = upper + factor * lax.shift_right_logical(words, 16).astype(jnp.float32)
            lower = lower + factor * (words & 65535).astype(jnp.float32)
        total = jnp.maximum(total, 1e-30)
        inverse = 1.0 / total
        return upper * inverse, lower * inverse, jnp.maximum(peak + jnp.log(total), NONE)

    def softmax(n):
        dz, dy = offsets(n)
        owner_at = behind(n)
        a, b = tab[0, owner_at * 2] & 31, tab[0, owner_at * 2 + 1] & 31
        first_a, second_a, first_b, second_b = tab[1, a], tab[2, a], tab[1, b], tab[2, b]
        codes = (
            jnp.where(first_a > 0, first_a, first_b),
            jnp.where(second_a > 0, second_a, jnp.where(first_a > 0, first_b, second_b)),
        )
        rows = (jnp.where(first_a > 0, 0, 1), jnp.where(second_a > 0, 0, 1))
        found = []
        for code, row in zip(codes, rows):
            q = jnp.where(row == 1, q_all[n, 1], q_all[n, 0])
            found.append((row, *page_part(code & 15, lax.shift_right_logical(code, 4), q)))
        values = []
        for r in range(2):
            tops = [jnp.where(row == r, top, LOW) for row, top, _, _ in found]
            peak = jnp.maximum(tops[0], tops[1])
            factors = [jnp.where(row == r, jnp.exp(t - peak), 0.0) for t, (row, _, _, _) in zip(tops, found)]
            total = jnp.maximum(factors[0] * found[0][2] + factors[1] * found[1][2], 1e-30)
            inverse = 1.0 / total
            value = (factors[0] * inverse) * found[0][3] + (factors[1] * inverse) * found[1][3]
            values.append((value, jnp.maximum(peak + jnp.log(total), NONE)))
        for h in range(2):
            part_send[h, dz * 4 + dy] = encode(
                [(v[32 * h:32 * h + 32], v[64 + 32 * h:96 + 32 * h], level) for v, level in values]
            )

    fetch_pool.wait()
    fill_tab.wait()

    def lightning_pair(p, carry):
        for n in (2 * p, 2 * p + 1):
            lightning(n)
        for n in (2 * p, 2 * p + 1):

            @pl.when(n > 0)
            def _(n=n):
                lin_back(n).start()

        return carry

    def pair(p, carry):
        for n in (2 * p, 2 * p + 1):
            dz, dy = offsets(n)

            @pl.when(dy > 0)
            def _(n=n):
                half(0, 0, n, at_offset(1, 0)).wait_recv()

            @pl.when(dz > 0)
            def _(n=n):
                half(1, 0, n, at_offset(1, 0)).wait_recv()

        for n in (2 * p, 2 * p + 1):
            softmax(n)
        for n in (2 * p, 2 * p + 1):
            dz, dy = offsets(n)

            @pl.when(dz > 0)
            def _(dz=dz, dy=dy):
                part(0, dz, dy).start()

            @pl.when(dy > 0)
            def _(dz=dz, dy=dy):
                part(1, dz, dy).start()

        return carry

    lax.fori_loop(0, 8, pair, 0)
    own_last.wait()
    for copy in lasts:
        copy.wait_recv()
    fetch_state.wait()
    lax.fori_loop(0, 8, lightning_pair, 0)

    step = lax.broadcasted_iota(jnp.int32, (1, WIDTH), 1) % 2

    def by_head(x):
        return jnp.concatenate(
            [jnp.broadcast_to(x[:, c * WIDTH:(c + 1) * WIDTH], (16, WIDTH)) for c in range(KVH)], axis=0
        ).T

    fresh = []
    for r in range(2):
        q = q_all[0, r].astype(jnp.float32)
        kv = [nkv[r, t].astype(jnp.float32) for t in range(2)]
        s0 = jnp.sum(q * by_head(kv[0][0:1]), axis=0, keepdims=True) * SCALE
        s1 = jnp.sum(q * by_head(kv[1][0:1]), axis=0, keepdims=True) * SCALE
        top = jnp.where(step == 1, jnp.maximum(s0, s1), s0)
        w0 = jnp.exp(s0 - top)
        w1 = jnp.where(step == 1, jnp.exp(s1 - top), 0.0)
        r0 = w0.astype(jnp.bfloat16).astype(jnp.float32)
        r1 = w1.astype(jnp.bfloat16).astype(jnp.float32)
        value = (r0 * by_head(kv[0][1:2]) + r1 * by_head(kv[1][1:2])) / (w0 + w1)
        fresh.append((value, top + jnp.log(w0 + w1)))

    def middle(k, carry):
        d = jnp.where(k < 3, 1 + 2 * k - 3 * (k // 2), 0)
        for h in range(2):
            for e in range(1, 4):
                part(h, e if h == 0 else d, d if h == 0 else e).wait_recv()
        for h in range(2):
            sources = [part_send[h, d if h == 0 else d * 4]]
            sources += [part_in[h, e * 4 + d if h == 0 else d * 4 + e] for e in range(1, 4)]
            mid_send[h, d] = encode([merged(sources, r) for r in range(2)])

        @pl.when(d > 0)
        def _():
            for h in range(2):
                last(h, d).start()

        return carry

    lax.fori_loop(0, 4, middle, 0)
    for h in range(2):
        for d in DIST:
            last(h, d).wait_recv()
    for r in range(2):
        pieces = []
        for h in range(2):
            value, level = fresh[r]
            sources = [mid_send[h, 0]] + [mid_in[h, d] for d in DIST]
            pieces.append(merged(sources, r, (value[32 * h:32 * h + 32], value[64 + 32 * h:96 + 32 * h], level)))
        soft_ref[r] = jnp.concatenate([pieces[0][0], pieces[1][0], pieces[0][1], pieces[1][1]], axis=0).T

    def finish(n, carry):
        half(0, 0, n, at_offset(1, 0)).wait_send()
        half(1, 0, n, at_offset(1, 0)).wait_send()
        lin = lin_back(n)
        lin.wait_recv()
        lin.wait_send()
        dz, dy = offsets(n)

        @pl.when(dz > 0)
        def _():
            part(0, dz, dy).wait_send()

        @pl.when(dy > 0)
        def _():
            part(1, dz, dy).wait_send()

        return carry

    lax.fori_loop(1, N, finish, 0)
    for copy in mids + lasts + [last(h, d) for h in range(2) for d in DIST]:
        copy.wait_send()

    def place(n, carry):
        dz, dy = offsets(n)
        rows = pl.ds(pl.multiple_of(at_offset(dz, dy) * 8, 8), 8)
        for r in range(2):
            lin_out[r, rows] = lin_in[n, r]
        return carry

    for r in range(2):
        lin_out[r, pl.ds(pl.multiple_of(me * 8, 8), 8)] = lin_send[0, r]
    lax.fori_loop(1, N, place, 0)
    for r in range(2):
        y = lin_fresh[2] * lin_out[r] + lin_fresh[r]
        lin_ref[r] = y / jnp.sqrt(jnp.mean(y * y, axis=1, keepdims=True) + 1e-5)


def copy_kernel(a_ref, b_ref, c_ref, d_ref):
    c_ref[...] = a_ref[...]
    d_ref[...] = b_ref[...]


def rows_first(x):
    return x.reshape(2, 2, 64, WIDTH).transpose(0, 2, 1, 3).reshape(2, WIDTH, WIDTH)


def pairs_first(x):
    return x.reshape(2, 2, 2, 64, WIDTH).transpose(0, 1, 3, 2, 4).reshape(2, 2, WIDTH, WIDTH)


def rows_last(x):
    return x.reshape(2, 64, 2, WIDTH).transpose(0, 2, 1, 3).reshape(2, 2, 64 * WIDTH)


def shards(
    request_owner, page_list, context_len, lin_state, decay_rate, lin_query, lin_keyval, soft_query, new_keyval,
    page_pool,
):
    vmem = pl.BlockSpec(memory_space=pltpu.VMEM)
    hbm = pl.BlockSpec(memory_space=pl.ANY)
    out = [jax.ShapeDtypeStruct((2, WIDTH, WIDTH), jnp.float32)] * 2
    lin, soft = pl.pallas_call(
        kernel,
        out_shape=out,
        in_specs=[vmem] * 4 + [hbm] * 6,
        out_specs=[vmem] * 2,
        scratch_shapes=[
            pltpu.VMEM(lin_state.shape, jnp.float32),
            pltpu.VMEM(page_pool.shape, jnp.bfloat16),
            pltpu.VMEM((2, WIDTH, WIDTH), jnp.bfloat16),
            pltpu.VMEM(new_keyval.shape, jnp.bfloat16),
            pltpu.VMEM((2, WIDTH, WIDTH), jnp.bfloat16),
            pltpu.VMEM((2, 2, WIDTH, WIDTH), jnp.bfloat16),
            pltpu.VMEM((3, WIDTH, WIDTH), jnp.float32),
            pltpu.VMEM((2, WIDTH, WIDTH), jnp.float32),
            pltpu.VMEM((N, 2, WIDTH, WIDTH), jnp.bfloat16),
            pltpu.VMEM((4, 4, 16, WIDTH), jnp.bfloat16),
            pltpu.VMEM((4, 4, 16, WIDTH), jnp.bfloat16),
            pltpu.VMEM((4, 4, 16, WIDTH), jnp.bfloat16),
            pltpu.VMEM((N, 2, 8, WIDTH), jnp.float32),
            pltpu.VMEM((N, 2, 8, WIDTH), jnp.float32),
            pltpu.VMEM((2, N, 72, WIDTH), jnp.int32),
            pltpu.VMEM((2, N, 72, WIDTH), jnp.int32),
            pltpu.VMEM((2, 4, 72, WIDTH), jnp.int32),
            pltpu.VMEM((2, 4, 72, WIDTH), jnp.int32),
            pltpu.VMEM((8, WIDTH), jnp.int32),
            pltpu.SMEM((8, WIDTH), jnp.int32),
            pltpu.SemaphoreType.DMA((9,)),
            pltpu.SemaphoreType.DMA((2, N)),
            pltpu.SemaphoreType.DMA((2, N)),
            pltpu.SemaphoreType.DMA((2, 4)),
            pltpu.SemaphoreType.DMA((2, 4)),
            pltpu.SemaphoreType.DMA((N,)),
            pltpu.SemaphoreType.DMA((N,)),
            pltpu.SemaphoreType.DMA((2, N)),
            pltpu.SemaphoreType.DMA((2, N)),
            pltpu.SemaphoreType.DMA((2, 4)),
            pltpu.SemaphoreType.DMA((2, 4)),
        ],
        compiler_params=pltpu.CompilerParams(
            collective_id=0, has_side_effects=True, vmem_limit_bytes=56 * 1024 * 1024
        ),
    )(
        request_owner.reshape(1, 32), page_list.T, context_len.reshape(1, 32), decay_rate.reshape(1, 64),
        rows_first(soft_query), new_keyval, rows_first(lin_query), pairs_first(lin_keyval), lin_state, page_pool,
    )
    lin, soft = pl.pallas_call(copy_kernel, out_shape=out, in_specs=[vmem] * 2, out_specs=[vmem] * 2)(lin, soft)
    return rows_last(lin), rows_last(soft)


def solution(mesh):
    return jax.shard_map(
        shards,
        mesh=mesh,
        in_specs=(
            P("grp"), P("grp", None), P("grp"), P("grp", "head", None, None), P(),
            P(("grp", "head"), None, None), P(("grp", "head"), None, None, None),
            P(("grp", "head"), None, None), P(("grp", "head"), None, None, None),
            P(("grp", "head"), None, None, None),
        ),
        out_specs=(P(("grp", "head"), None, None), P(("grp", "head"), None, None)),
        check_vma=False,
    )
```

time: 40.2 us -> 37.2 us (0.925)
  Pallas kernels: 39.3 us -> 36.4 us
    pallas_call x1, Pallas kernels: 37.7 us -> 34.7 us  [shards(): pl.pallas_call(kernel, out_shape=out, in_specs=[vmem] * 4 + [hbm] * 6, ou...]
where the time goes in v3:
time: 37.2 us; the launch traced here: 37.1 us
  Pallas kernels  36.4 us (98%)
  between operations  0.64 us (2%)
    pallas_call x1, Pallas kernels, shards(): pl.pallas_call(kernel, out_shape=out, in_specs=[vmem] * 4 + [hbm] * 6, ou...  34.7 us
    pallas_call x1, Pallas kernels, shards(): pl.pallas_call(copy_kernel, out_shape=out, in_specs=[vmem] * 2, out_specs...  1.68 us

profile of v3, /device:TPU:0, one launch (start us, length us, event | category | flops | bytes accessed | tf_op | source)
XLA Modules:
  0.0 37.1 jit_solution(14517058594018154521)
XLA Ops:
  0.6 34.7 %shard_map.113 = (f32[2,128,128]{2,1,0:T(8,128)}, f32[2,128,128]{2,1,0:T(8,128)}) custom-call(s32[1,32]{1,0:T(1,128)} %bitcast.33, s32[8,32]{1,0:T(8,128)} %bitcast.32, s32[1,32]{1,0:T(1,128)} %bitcast.34, f32[1,64]{1,0:T(1,128)} %bitcast.35, bf16[2,128,128]{2,1,0:T(8,128)(2,1)} %bitcast.30, bf16[2,2,2,1024]{3,2,1,0:T(2,128)(2,1)} %nkv_hbm.1, ...), custom_call_target="tpu_custom_call" | custom-call | tf_op jit(solution)/shard_map/pallas_call | solution.py:450
  35.4 1.7 %shard_map.114 = (f32[2,128,128]{2,1,0:T(8,128)}, f32[2,128,128]{2,1,0:T(8,128)}) custom-call(f32[2,128,128]{2,1,0:T(8,128)} %get-tuple-element.6.a_ref, f32[2,128,128]{2,1,0:T(8,128)} %get-tuple-element.7.b_ref), custom_call_target="tpu_custom_call" | custom-call | tf_op jit(solution)/shard_map/pallas_call | solution.py:495

commit v4 on v3

--- a/solution.py
+++ b/solution.py
@@ -21,7 +21,7 @@
 
 
 DIST = (1, 3, 2)
-OFFSETS = ((0, 0), (1, 0), (0, 1), (3, 0), (0, 3), (2, 0), (0, 2), (1, 1), (1, 3), (3, 1), (3, 3), (1, 2), (2, 1), (3, 2), (2, 3), (2, 2))
+OFFSETS = ((0, 0), (1, 0), (0, 1), (3, 0), (0, 3), (2, 0), (0, 2), (1, 1), (1, 3), (3, 1), (1, 2), (2, 1), (3, 3), (3, 2), (2, 3), (2, 2))
 SLOT = {offset: n for n, offset in enumerate(OFFSETS)}
 
 
@@ -54,7 +54,7 @@
 
 def kernel(
     owner, pages, length, rate, sq_hbm, nkv_hbm, lq_hbm, lkv_hbm, state_hbm, pool_hbm, lin_ref, soft_ref,
-    state, pool, sq, nkv, lq, lkv, lin_fresh, lin_out, q_all, lin_pack, lin_mid, lin_all, lin_send, lin_in, part_send, part_in, mid_send, mid_in,
+    state, pool, sq, nkv, lq, lkv, lin_fresh, lin_out, fresh, fresh_log, q_all, lin_pack, lin_mid, lin_all, lin_send, lin_in, part_send, part_in, mid_send, mid_in,
     tab_rows, tab, local_sem, half_send, half_recv, mid_sems, mid_recvs, back_send, back_recv,
     part_sems, part_recvs, last_sems, last_recvs,
 ):
@@ -142,6 +142,25 @@
         qk2 = jnp.sum(wide[r] * k2, axis=1, keepdims=True)
         lin_fresh[r] = (lam_first * qk1) * v1 + (lam_second * qk2) * v2
     lin_fresh[2] = jnp.broadcast_to(lam_state, (WIDTH, WIDTH))
+    step = lax.broadcasted_iota(jnp.int32, (1, WIDTH), 1) % 2
+
+    def by_head(x):
+        return jnp.concatenate(
+            [jnp.broadcast_to(x[:, c * WIDTH:(c + 1) * WIDTH], (16, WIDTH)) for c in range(KVH)], axis=0
+        ).T
+
+    for r in range(2):
+        q = q_all[0, r].astype(jnp.float32)
+        kv = [nkv[r, t].astype(jnp.float32) for t in range(2)]
+        s0 = jnp.sum(q * by_head(kv[0][0:1]), axis=0, keepdims=True) * SCALE
+        s1 = jnp.sum(q * by_head(kv[1][0:1]), axis=0, keepdims=True) * SCALE
+        top = jnp.where(step == 1, jnp.maximum(s0, s1), s0)
+        w0 = jnp.exp(s0 - top)
+        w1 = jnp.where(step == 1, jnp.exp(s1 - top), 0.0)
+        r0 = w0.astype(jnp.bfloat16).astype(jnp.float32)
+        r1 = w1.astype(jnp.bfloat16).astype(jnp.float32)
+        fresh[r] = (r0 * by_head(kv[0][1:2]) + r1 * by_head(kv[1][1:2])) / (w0 + w1)
+        fresh_log[r:r + 1] = top + jnp.log(w0 + w1)
     pl.semaphore_wait(barrier, 6)
 
     mids = [
@@ -173,13 +192,14 @@
         copy.start()
     own_last = pltpu.make_async_copy(lin_mid.at[:, my], lin_all.at[0], local_sem.at[3])
     own_last.start()
-    for d in DIST:
-        first[0, d].wait_recv()
-        for e in DIST:
-            half(0, SLOT[d, 0], SLOT[d, e], at_offset(0, e)).start()
-        first[1, d].wait_recv()
-        for e in DIST:
-            half(1, SLOT[0, d], SLOT[e, d], at_offset(e, 0)).start()
+    here = set()
+    for dz, dy in OFFSETS[7:]:
+        for h, d in ((0, dz), (1, dy)):
+            if (h, d) not in here:
+                first[h, d].wait_recv()
+                here.add((h, d))
+        half(0, SLOT[dz, 0], SLOT[dz, dy], at_offset(0, dy)).start()
+        half(1, SLOT[0, dy], SLOT[dz, dy], at_offset(dz, 0)).start()
 
     head_of = lax.broadcasted_iota(jnp.int32, (8, WIDTH), 0) // 2
 
@@ -237,7 +257,7 @@
             low = (lower * inverse + 32768.5).astype(jnp.int32)
             words.append(lax.shift_left(high, 16) | low)
             logs += [(level * LEVEL_UNIT).astype(jnp.int32), size.astype(jnp.int32)]
-        return jnp.concatenate(words + logs + [jnp.zeros((4, WIDTH), jnp.int32)], axis=0)
+        return jnp.concatenate(words + logs, axis=0)
 
     def merged(sources, r, more=None):
         levels = [x[64 + 2 * r:65 + 2 * r].astype(jnp.float32) * (1.0 / LEVEL_UNIT) for x in sources]
@@ -336,27 +356,6 @@
     fetch_state.wait()
     lax.fori_loop(0, 8, lightning_pair, 0)
 
-    step = lax.broadcasted_iota(jnp.int32, (1, WIDTH), 1) % 2
-
-    def by_head(x):
-        return jnp.concatenate(
-            [jnp.broadcast_to(x[:, c * WIDTH:(c + 1) * WIDTH], (16, WIDTH)) for c in range(KVH)], axis=0
-        ).T
-
-    fresh = []
-    for r in range(2):
-        q = q_all[0, r].astype(jnp.float32)
-        kv = [nkv[r, t].astype(jnp.float32) for t in range(2)]
-        s0 = jnp.sum(q * by_head(kv[0][0:1]), axis=0, keepdims=True) * SCALE
-        s1 = jnp.sum(q * by_head(kv[1][0:1]), axis=0, keepdims=True) * SCALE
-        top = jnp.where(step == 1, jnp.maximum(s0, s1), s0)
-        w0 = jnp.exp(s0 - top)
-        w1 = jnp.where(step == 1, jnp.exp(s1 - top), 0.0)
-        r0 = w0.astype(jnp.bfloat16).astype(jnp.float32)
-        r1 = w1.astype(jnp.bfloat16).astype(jnp.float32)
-        value = (r0 * by_head(kv[0][1:2]) + r1 * by_head(kv[1][1:2])) / (w0 + w1)
-        fresh.append((value, top + jnp.log(w0 + w1)))
-
     def middle(k, carry):
         d = jnp.where(k < 3, 1 + 2 * k - 3 * (k // 2), 0)
         for h in range(2):
@@ -375,13 +374,29 @@
         return carry
 
     lax.fori_loop(0, 4, middle, 0)
+
+    def place(n, carry):
+        lin_back(n).wait_recv()
+        dz, dy = offsets(n)
+        rows = pl.ds(pl.multiple_of(at_offset(dz, dy) * 8, 8), 8)
+        for r in range(2):
+            lin_out[r, rows] = lin_in[n, r]
+        return carry
+
+    for r in range(2):
+        lin_out[r, pl.ds(pl.multiple_of(me * 8, 8), 8)] = lin_send[0, r]
+    lax.fori_loop(1, N, place, 0)
+    for r in range(2):
+        y = lin_fresh[2] * lin_out[r] + lin_fresh[r]
+        lin_ref[r] = y / jnp.sqrt(jnp.mean(y * y, axis=1, keepdims=True) + 1e-5)
+
     for h in range(2):
         for d in DIST:
             last(h, d).wait_recv()
     for r in range(2):
         pieces = []
         for h in range(2):
-            value, level = fresh[r]
+            value, level = fresh[r], fresh_log[r:r + 1]
             sources = [mid_send[h, 0]] + [mid_in[h, d] for d in DIST]
             pieces.append(merged(sources, r, (value[32 * h:32 * h + 32], value[64 + 32 * h:96 + 32 * h], level)))
         soft_ref[r] = jnp.concatenate([pieces[0][0], pieces[1][0], pieces[0][1], pieces[1][1]], axis=0).T
@@ -389,9 +404,7 @@
     def finish(n, carry):
         half(0, 0, n, at_offset(1, 0)).wait_send()
         half(1, 0, n, at_offset(1, 0)).wait_send()
-        lin = lin_back(n)
-        lin.wait_recv()
-        lin.wait_send()
+        lin_back(n).wait_send()
         dz, dy = offsets(n)
 
         @pl.when(dz > 0)
@@ -407,20 +420,6 @@
     lax.fori_loop(1, N, finish, 0)
     for copy in mids + lasts + [last(h, d) for h in range(2) for d in DIST]:
         copy.wait_send()
-
-    def place(n, carry):
-        dz, dy = offsets(n)
-        rows = pl.ds(pl.multiple_of(at_offset(dz, dy) * 8, 8), 8)
-        for r in range(2):
-            lin_out[r, rows] = lin_in[n, r]
-        return carry
-
-    for r in range(2):
-        lin_out[r, pl.ds(pl.multiple_of(me * 8, 8), 8)] = lin_send[0, r]
-    lax.fori_loop(1, N, place, 0)
-    for r in range(2):
-        y = lin_fresh[2] * lin_out[r] + lin_fresh[r]
-        lin_ref[r] = y / jnp.sqrt(jnp.mean(y * y, axis=1, keepdims=True) + 1e-5)
 
 
 def copy_kernel(a_ref, b_ref, c_ref, d_ref):
@@ -449,7 +448,7 @@
     out = [jax.ShapeDtypeStruct((2, WIDTH, WIDTH), jnp.float32)] * 2
     lin, soft = pl.pallas_call(
         kernel,
-        out_shape=out,
+        out_shape=[pltpu.VMEM((2, WIDTH, WIDTH), jnp.float32)] * 2,
         in_specs=[vmem] * 4 + [hbm] * 6,
         out_specs=[vmem] * 2,
         scratch_shapes=[
@@ -461,16 +460,18 @@
             pltpu.VMEM((2, 2, WIDTH, WIDTH), jnp.bfloat16),
             pltpu.VMEM((3, WIDTH, WIDTH), jnp.float32),
             pltpu.VMEM((2, WIDTH, WIDTH), jnp.float32),
+            pltpu.VMEM((2, WIDTH, WIDTH), jnp.float32),
+            pltpu.VMEM((8, WIDTH), jnp.float32),
             pltpu.VMEM((N, 2, WIDTH, WIDTH), jnp.bfloat16),
             pltpu.VMEM((4, 4, 16, WIDTH), jnp.bfloat16),
             pltpu.VMEM((4, 4, 16, WIDTH), jnp.bfloat16),
             pltpu.VMEM((4, 4, 16, WIDTH), jnp.bfloat16),
             pltpu.VMEM((N, 2, 8, WIDTH), jnp.float32),
             pltpu.VMEM((N, 2, 8, WIDTH), jnp.float32),
-            pltpu.VMEM((2, N, 72, WIDTH), jnp.int32),
-            pltpu.VMEM((2, N, 72, WIDTH), jnp.int32),
-            pltpu.VMEM((2, 4, 72, WIDTH), jnp.int32),
-            pltpu.VMEM((2, 4, 72, WIDTH), jnp.int32),
+            pltpu.VMEM((2, N, 68, WIDTH), jnp.int32),
+            pltpu.VMEM((2, N, 68, WIDTH), jnp.int32),
+            pltpu.VMEM((2, 4, 68, WIDTH), jnp.int32),
+            pltpu.VMEM((2, 4, 68, WIDTH), jnp.int32),
             pltpu.VMEM((8, WIDTH), jnp.int32),
             pltpu.SMEM((8, WIDTH), jnp.int32),
             pltpu.SemaphoreType.DMA((9,)),
@@ -492,6 +493,7 @@
         request_owner.reshape(1, 32), page_list.T, context_len.reshape(1, 32), decay_rate.reshape(1, 64),
         rows_first(soft_query), new_keyval, rows_first(lin_query), pairs_first(lin_keyval), lin_state, page_pool,
     )
+    lin, soft = (pltpu.with_memory_space_constraint(x, pltpu.VMEM) for x in (lin, soft))
     lin, soft = pl.pallas_call(copy_kernel, out_shape=out, in_specs=[vmem] * 2, out_specs=[vmem] * 2)(lin, soft)
     return rows_last(lin), rows_last(soft)
 

time: 37.2 us -> 33.4 us (0.90)
  Pallas kernels: 36.4 us -> 32.6 us
    pallas_call x1, Pallas kernels: 34.7 us -> 31.9 us  [shards(): pl.pallas_call(kernel, out_shape=[pltpu.VMEM((2, WIDTH, WIDTH), jnp.float...]
    pallas_call x1, Pallas kernels: 1.68 us -> 0.72 us  [shards(): pl.pallas_call(copy_kernel, out_shape=out, in_specs=[vmem] * 2, out_specs...]
where the time goes in v4:
time: 33.4 us; the launch traced here: 33.3 us
  Pallas kernels  32.6 us (98%)
  between operations  0.64 us (2%)
    pallas_call x1, Pallas kernels, shards(): pl.pallas_call(kernel, out_shape=[pltpu.VMEM((2, WIDTH, WIDTH), jnp.float...  31.9 us
    pallas_call x1, Pallas kernels, shards(): pl.pallas_call(copy_kernel, out_shape=out, in_specs=[vmem] * 2, out_specs...  0.72 us

profile of v4, /device:TPU:0, one launch (start us, length us, event | category | flops | bytes accessed | tf_op | source)
XLA Modules:
  0.0 33.3 jit_solution(17121287285866224788)
XLA Ops:
  0.6 31.9 %shard_map.113 = (f32[2,128,128]{2,1,0:T(8,128)S(1)}, f32[2,128,128]{2,1,0:T(8,128)S(1)}) custom-call(s32[1,32]{1,0:T(1,128)} %bitcast.33, s32[8,32]{1,0:T(8,128)} %bitcast.32, s32[1,32]{1,0:T(1,128)} %bitcast.34, f32[1,64]{1,0:T(1,128)} %bitcast.35, bf16[2,128,128]{2,1,0:T(8,128)(2,1)} %bitcast.30, bf16[2,2,2,1024]{3,2,1,0:T(2,128)(2,1)} %nkv_hbm.1, ...), custom_call_target="tpu_custom_call" | custom-call | tf_op jit(solution)/shard_map/pallas_call | solution.py:449
  32.6 0.7 %shard_map.114 = (f32[2,128,128]{2,1,0:T(8,128)}, f32[2,128,128]{2,1,0:T(8,128)}) custom-call(f32[2,128,128]{2,1,0:T(8,128)S(1)} %get-tuple-element.6.a_ref, f32[2,128,128]{2,1,0:T(8,128)S(1)} %get-tuple-element.7.b_ref), custom_call_target="tpu_custom_call" | custom-call | tf_op jit(solution)/shard_map/pallas_call | solution.py:497

commit v5 on v4

--- a/solution.py
+++ b/solution.py
@@ -25,10 +25,13 @@
 SLOT = {offset: n for n, offset in enumerate(OFFSETS)}
 
 
+def packed(axis):
+    bits = sum(offset[axis] << 2 * n for n, offset in enumerate(OFFSETS))
+    return bits - (1 << 32) if bits >= 1 << 31 else bits
+
+
 def offsets(n):
-    return tuple(
-        sum(jnp.where(n == i, offset[axis], 0) for i, offset in enumerate(OFFSETS) if offset[axis]) for axis in (0, 1)
-    )
+    return tuple(lax.shift_right_logical(jnp.int32(packed(axis)), jnp.int32(2 * n)) & 3 for axis in (0, 1))
 
 
 def make_tables(owner, pages, length, me):
@@ -53,8 +56,8 @@
 
 
 def kernel(
-    owner, pages, length, rate, sq_hbm, nkv_hbm, lq_hbm, lkv_hbm, state_hbm, pool_hbm, lin_ref, soft_ref,
-    state, pool, sq, nkv, lq, lkv, lin_fresh, lin_out, fresh, fresh_log, q_all, lin_pack, lin_mid, lin_all, lin_send, lin_in, part_send, part_in, mid_send, mid_in,
+    owner_hbm, pages_hbm, length_hbm, rate_hbm, sq_hbm, nkv_hbm, lq_hbm, lkv_hbm, state_hbm, pool_hbm, lin_ref, soft_ref,
+    state, pool, owner, pages, length, rate, sq, nkv, lq, lkv, lin_fresh, lin_out, fresh, fresh_log, q_all, lin_pack, lin_mid, lin_all, lin_send, lin_in, part_send, part_in, mid_send, mid_in,
     tab_rows, tab, local_sem, half_send, half_recv, mid_sems, mid_recvs, back_send, back_recv,
     part_sems, part_recvs, last_sems, last_recvs,
 ):
@@ -97,7 +100,12 @@
             pl.semaphore_signal(barrier, inc=1, device_id={"head": to}, device_id_type=MESH)
     loads = [
         pltpu.make_async_copy(src, dst, local_sem.at[5 + n])
-        for n, (src, dst) in enumerate(((sq_hbm, sq), (lq_hbm, lq), (lkv_hbm, lkv), (nkv_hbm, nkv)))
+        for n, (src, dst) in enumerate(
+            (
+                (owner_hbm, owner), (pages_hbm, pages), (length_hbm, length), (rate_hbm, rate),
+                (sq_hbm, sq), (lq_hbm, lq), (lkv_hbm, lkv), (nkv_hbm, nkv),
+            )
+        )
     ]
     for copy in loads:
         copy.start()
@@ -105,13 +113,13 @@
     fetch_state = pltpu.make_async_copy(state_hbm, state, local_sem.at[0])
     fetch_pool.start()
     fetch_state.start()
+    for copy in loads:
+        copy.wait()
     tab_rows[...] = jnp.zeros((8, WIDTH), jnp.int32)
     for n, row in enumerate(make_tables(owner[...], pages[...], length[...], me)):
         tab_rows[n:n + 1, 0:32] = row
     fill_tab = pltpu.make_async_copy(tab_rows, tab, local_sem.at[4])
     fill_tab.start()
-    for copy in loads:
-        copy.wait()
     wide = [lq[r].astype(jnp.float32) for r in range(2)]
     for peer in range(N):
         lin_pack[peer // 4, peer % 4] = jnp.concatenate(
@@ -449,11 +457,15 @@
     lin, soft = pl.pallas_call(
         kernel,
         out_shape=[pltpu.VMEM((2, WIDTH, WIDTH), jnp.float32)] * 2,
-        in_specs=[vmem] * 4 + [hbm] * 6,
+        in_specs=[hbm] * 10,
         out_specs=[vmem] * 2,
         scratch_shapes=[
             pltpu.VMEM(lin_state.shape, jnp.float32),
             pltpu.VMEM(page_pool.shape, jnp.bfloat16),
+            pltpu.VMEM((1, 32), jnp.int32),
+            pltpu.VMEM((8, 32), jnp.int32),
+            pltpu.VMEM((1, 32), jnp.int32),
+            pltpu.VMEM((1, 64), jnp.float32),
             pltpu.VMEM((2, WIDTH, WIDTH), jnp.bfloat16),
             pltpu.VMEM(new_keyval.shape, jnp.bfloat16),
             pltpu.VMEM((2, WIDTH, WIDTH), jnp.bfloat16),
@@ -474,7 +486,7 @@
             pltpu.VMEM((2, 4, 68, WIDTH), jnp.int32),
             pltpu.VMEM((8, WIDTH), jnp.int32),
             pltpu.SMEM((8, WIDTH), jnp.int32),
-            pltpu.SemaphoreType.DMA((9,)),
+            pltpu.SemaphoreType.DMA((13,)),
             pltpu.SemaphoreType.DMA((2, N)),
             pltpu.SemaphoreType.DMA((2, N)),
             pltpu.SemaphoreType.DMA((2, 4)),

time: 33.4 us -> 32.3 us (0.967)
  Pallas kernels: 32.6 us -> 31.5 us
    pallas_call x1, Pallas kernels: 31.9 us -> 30.8 us  [shards(): pl.pallas_call(kernel, out_shape=[pltpu.VMEM((2, WIDTH, WIDTH), jnp.float...]
where the time goes in v5:
time: 32.3 us; the launch traced here: 32.2 us
  Pallas kernels  31.5 us (98%)
  between operations  0.64 us (2%)
    pallas_call x1, Pallas kernels, shards(): pl.pallas_call(kernel, out_shape=[pltpu.VMEM((2, WIDTH, WIDTH), jnp.float...  30.8 us
    pallas_call x1, Pallas kernels, shards(): pl.pallas_call(copy_kernel, out_shape=out, in_specs=[vmem] * 2, out_specs...  0.72 us

profile of v5, /device:TPU:0, one launch (start us, length us, event | category | flops | bytes accessed | tf_op | source)
XLA Modules:
  0.0 32.2 jit_solution(14825589843009140733)
XLA Ops:
  0.6 30.8 %shard_map.113 = (f32[2,128,128]{2,1,0:T(8,128)S(1)}, f32[2,128,128]{2,1,0:T(8,128)S(1)}) custom-call(s32[1,32]{1,0:T(1,128)} %bitcast.33, s32[8,32]{1,0:T(8,128)} %bitcast.32, s32[1,32]{1,0:T(1,128)} %bitcast.34, f32[1,64]{1,0:T(1,128)} %bitcast.35, bf16[2,128,128]{2,1,0:T(8,128)(2,1)} %bitcast.30, bf16[2,2,2,1024]{3,2,1,0:T(2,128)(2,1)} %nkv_hbm.1, ...), custom_call_target="tpu_custom_call" | custom-call | tf_op jit(solution)/shard_map/pallas_call | solution.py:457
  31.4 0.7 %shard_map.114 = (f32[2,128,128]{2,1,0:T(8,128)}, f32[2,128,128]{2,1,0:T(8,128)}) custom-call(f32[2,128,128]{2,1,0:T(8,128)S(1)} %get-tuple-element.6.a_ref, f32[2,128,128]{2,1,0:T(8,128)S(1)} %get-tuple-element.7.b_ref), custom_call_target="tpu_custom_call" | custom-call | tf_op jit(solution)/shard_map/pallas_call | solution.py:509

commit v6 on v5

--- a/solution.py
+++ b/solution.py
@@ -369,14 +369,12 @@
         for h in range(2):
             for e in range(1, 4):
                 part(h, e if h == 0 else d, d if h == 0 else e).wait_recv()
-        for h in range(2):
             sources = [part_send[h, d if h == 0 else d * 4]]
             sources += [part_in[h, e * 4 + d if h == 0 else d * 4 + e] for e in range(1, 4)]
             mid_send[h, d] = encode([merged(sources, r) for r in range(2)])
 
-        @pl.when(d > 0)
-        def _():
-            for h in range(2):
+            @pl.when(d > 0)
+            def _(h=h):
                 last(h, d).start()
 
         return carry
@@ -397,6 +395,26 @@
     for r in range(2):
         y = lin_fresh[2] * lin_out[r] + lin_fresh[r]
         lin_ref[r] = y / jnp.sqrt(jnp.mean(y * y, axis=1, keepdims=True) + 1e-5)
+
+    def finish(n, carry):
+        half(0, 0, n, at_offset(1, 0)).wait_send()
+        half(1, 0, n, at_offset(1, 0)).wait_send()
+        lin_back(n).wait_send()
+        dz, dy = offsets(n)
+
+        @pl.when(dz > 0)
+        def _():
+            part(0, dz, dy).wait_send()
+
+        @pl.when(dy > 0)
+        def _():
+            part(1, dz, dy).wait_send()
+
+        return carry
+
+    lax.fori_loop(1, N, finish, 0)
+    for copy in mids + lasts:
+        copy.wait_send()
 
     for h in range(2):
         for d in DIST:
@@ -408,25 +426,7 @@
             sources = [mid_send[h, 0]] + [mid_in[h, d] for d in DIST]
             pieces.append(merged(sources, r, (value[32 * h:32 * h + 32], value[64 + 32 * h:96 + 32 * h], level)))
         soft_ref[r] = jnp.concatenate([pieces[0][0], pieces[1][0], pieces[0][1], pieces[1][1]], axis=0).T
-
-    def finish(n, carry):
-        half(0, 0, n, at_offset(1, 0)).wait_send()
-        half(1, 0, n, at_offset(1, 0)).wait_send()
-        lin_back(n).wait_send()
-        dz, dy = offsets(n)
-
-        @pl.when(dz > 0)
-        def _():
-            part(0, dz, dy).wait_send()
-
-        @pl.when(dy > 0)
-        def _():
-            part(1, dz, dy).wait_send()
-
-        return carry
-
-    lax.fori_loop(1, N, finish, 0)
-    for copy in mids + lasts + [last(h, d) for h in range(2) for d in DIST]:
+    for copy in [last(h, d) for h in range(2) for d in DIST]:
         copy.wait_send()
 
 

time: 32.3 us -> 32 us (level)
  no operation moved by 1% of the time
where the time goes in v6:
time: 32 us; the launch traced here: 31.9 us
  Pallas kernels  31.2 us (98%)
  between operations  0.64 us (2%)
    pallas_call x1, Pallas kernels, shards(): pl.pallas_call(kernel, out_shape=[pltpu.VMEM((2, WIDTH, WIDTH), jnp.float...  30.5 us
    pallas_call x1, Pallas kernels, shards(): pl.pallas_call(copy_kernel, out_shape=out, in_specs=[vmem] * 2, out_specs...  0.72 us

profile of v6, /device:TPU:0, one launch (start us, length us, event | category | flops | bytes accessed | tf_op | source)
XLA Modules:
  0.0 31.9 jit_solution(12547627087255606224)
XLA Ops:
  0.6 30.5 %shard_map.113 = (f32[2,128,128]{2,1,0:T(8,128)S(1)}, f32[2,128,128]{2,1,0:T(8,128)S(1)}) custom-call(s32[1,32]{1,0:T(1,128)} %bitcast.33, s32[8,32]{1,0:T(8,128)} %bitcast.32, s32[1,32]{1,0:T(1,128)} %bitcast.34, f32[1,64]{1,0:T(1,128)} %bitcast.35, bf16[2,128,128]{2,1,0:T(8,128)(2,1)} %bitcast.30, bf16[2,2,2,1024]{3,2,1,0:T(2,128)(2,1)} %nkv_hbm.1, ...), custom_call_target="tpu_custom_call" | custom-call | tf_op jit(solution)/shard_map/pallas_call | solution.py:457
  31.2 0.7 %shard_map.114 = (f32[2,128,128]{2,1,0:T(8,128)}, f32[2,128,128]{2,1,0:T(8,128)}) custom-call(f32[2,128,128]{2,1,0:T(8,128)S(1)} %get-tuple-element.6.a_ref, f32[2,128,128]{2,1,0:T(8,128)S(1)} %get-tuple-element.7.b_ref), custom_call_target="tpu_custom_call" | custom-call | tf_op jit(solution)/shard_map/pallas_call | solution.py:509

commit v7 on v6

--- a/solution.py
+++ b/solution.py
@@ -416,15 +416,22 @@
     for copy in mids + lasts:
         copy.wait_send()
 
+    own = []
+    for r in range(2):
+        value, level = fresh[r], fresh_log[r:r + 1]
+        own.append(
+            [
+                merged([mid_send[h, 0]], r, (value[32 * h:32 * h + 32], value[64 + 32 * h:96 + 32 * h], level))
+                for h in range(2)
+            ]
+        )
     for h in range(2):
         for d in DIST:
             last(h, d).wait_recv()
     for r in range(2):
         pieces = []
         for h in range(2):
-            value, level = fresh[r], fresh_log[r:r + 1]
-            sources = [mid_send[h, 0]] + [mid_in[h, d] for d in DIST]
-            pieces.append(merged(sources, r, (value[32 * h:32 * h + 32], value[64 + 32 * h:96 + 32 * h], level)))
+            pieces.append(merged([mid_in[h, d] for d in DIST], r, own[r][h]))
         soft_ref[r] = jnp.concatenate([pieces[0][0], pieces[1][0], pieces[0][1], pieces[1][1]], axis=0).T
     for copy in [last(h, d) for h in range(2) for d in DIST]:
         copy.wait_send()

time: 32 us -> 32 us (level)
  no operation moved by 1% of the time
where the time goes in v7:
time: 32 us; the launch traced here: 31.8 us
  Pallas kernels  31.2 us (98%)
  between operations  0.64 us (2%)
    pallas_call x1, Pallas kernels, shards(): pl.pallas_call(kernel, out_shape=[pltpu.VMEM((2, WIDTH, WIDTH), jnp.float...  30.5 us
    pallas_call x1, Pallas kernels, shards(): pl.pallas_call(copy_kernel, out_shape=out, in_specs=[vmem] * 2, out_specs...  0.72 us

profile of v7, /device:TPU:0, one launch (start us, length us, event | category | flops | bytes accessed | tf_op | source)
XLA Modules:
  0.0 31.8 jit_solution(5200806616480981445)
XLA Ops:
  0.6 30.5 %shard_map.113 = (f32[2,128,128]{2,1,0:T(8,128)S(1)}, f32[2,128,128]{2,1,0:T(8,128)S(1)}) custom-call(s32[1,32]{1,0:T(1,128)} %bitcast.33, s32[8,32]{1,0:T(8,128)} %bitcast.32, s32[1,32]{1,0:T(1,128)} %bitcast.34, f32[1,64]{1,0:T(1,128)} %bitcast.35, bf16[2,128,128]{2,1,0:T(8,128)(2,1)} %bitcast.30, bf16[2,2,2,1024]{3,2,1,0:T(2,128)(2,1)} %nkv_hbm.1, ...), custom_call_target="tpu_custom_call" | custom-call | tf_op jit(solution)/shard_map/pallas_call | solution.py:464
  31.1 0.7 %shard_map.114 = (f32[2,128,128]{2,1,0:T(8,128)}, f32[2,128,128]{2,1,0:T(8,128)}) custom-call(f32[2,128,128]{2,1,0:T(8,128)S(1)} %get-tuple-element.6.a_ref, f32[2,128,128]{2,1,0:T(8,128)S(1)} %get-tuple-element.7.b_ref), custom_call_target="tpu_custom_call" | custom-call | tf_op jit(solution)/shard_map/pallas_call | solution.py:516
